TPU v7x, 128 devices: a whole 4x4x4 slice. The times are simulated.
128 devices in a mesh: layer: 2 (over core), feat: 64 (over y, x, z).
Axes of the slice: x: 4, y: 4, z: 4, core: 2. Of those that a mesh axis runs over, the one named last changes fastest.
Arguments:
- inputs: bfloat16 [2, 512, 4608], P('layer', 'feat'), may hold values from -6 to 6
- targets: bfloat16 [2, 512, 4608], P('layer', 'feat'), may hold values from -6 to 6
- w_enc: bfloat16 [2, 4608, 32768], P('layer', None, 'feat'), may hold values from -0.09375 to 0.09375
- b_enc: float32 [2, 32768], P('layer', 'feat'), may hold values from -4 to 4
- w_self: bfloat16 [2, 32768, 4608], P('layer', 'feat'), may hold values from -0.1875 to 0.1875
- w_cross: bfloat16 [32768, 4608], P('feat', 'layer'), may hold values from -0.1875 to 0.1875
- block_ids: int32 [2, 512, 8], P('layer', 'feat'), may hold values from 0 to 255, all different within a row
Outputs:
- reconstruction: float32 [2, 512, 4608], P('layer', 'feat')
- active_codes: bfloat16 [2, 512, 8, 128], P('layer', 'feat')
- grad_enc: bfloat16 [2, 4608, 32768], P('layer', None, 'feat')
- grad_benc: float32 [2, 32768], P('layer', 'feat')
- grad_self: bfloat16 [2, 32768, 4608], P('layer', 'feat')
- grad_cross: bfloat16 [32768, 4608], P('feat', 'layer')
Inputs may be any that keep to these rules, and one draw needn't show every extreme that they name: `block_ids`: each token names 8 different blocks in each layer; every block is named by some token of the two layers taken together.
All inputs are finite; a program needn't handle non-finite values.
Results may differ from a plain program's by a relative error of at most 0.0058.
Values may be sent and summed in bfloat16 or wider, within the bound.
No kernel may reach another device: no remote copies, remote signals or barrier semaphores. Data moves between devices by JAX's collectives and lax.ppermute only.
A program may use at most 128 MiB of HBM per device.

v0:
```python
import functools

import jax
import jax.numpy as jnp
from jax import lax
from jax.experimental import pallas as pl
from jax.experimental.pallas import tpu as pltpu
from jax.sharding import PartitionSpec as P

BLK = 128
SIDE = 4
LINE = 32
PLANE = 128
CAP = 64
ROWS = SIDE * CAP
AWAY = (0, 2, 1, 3)
STEPS = {"y": (1, 0, 0), "x": (0, 1, 0), "z": (0, 0, 1)}
F32, BF16 = jnp.float32, jnp.bfloat16

OUTER = ("z", "y")
MIDDLE = ("x", "z")
INNER = ("y", "x")

PARAMS = pltpu.CompilerParams(vmem_limit_bytes=20 * 2**20)


def route(axes, distance):
    pairs = []
    for core, axis in enumerate(axes):
        step = STEPS[axis]
        for y in range(SIDE):
            for x in range(SIDE):
                for z in range(SIDE):
                    there = [(c + distance * s) % SIDE for c, s in zip((y, x, z), step)]
                    base = core * SIDE**3
                    pairs.append(
                        (base + (y * SIDE + x) * SIDE + z, base + (there[0] * SIDE + there[1]) * SIDE + there[2])
                    )
    return pairs


def send(block, axes, distance):
    return lax.ppermute(block, ("layer", "feat"), route(axes, distance))


def ahead(block, pieces, axes):
    return [block] + [send(pieces[r], axes, -AWAY[r]) for r in (1, 2, 3)]


def behind(pieces, axes):
    return [pieces[0]] + [send(pieces[r], axes, AWAY[r]) for r in (1, 2, 3)]


def to_second(block):
    return lax.ppermute(block, "layer", [(0, 1)])


def to_first(block):
    return lax.ppermute(block, "layer", [(1, 0)])


def swapped(block):
    return lax.ppermute(block, "layer", [(0, 1), (1, 0)])


def line_gather(block, axes):
    return ahead(block, [block] * SIDE, axes)


def line_reduce(terms, axes):
    terms = behind([terms[0]] + [term.astype(BF16) for term in terms[1:]], axes)
    return sum(term.astype(F32) for term in terms)


def contract_rows(left, right):
    return lax.dot_general(left, right, (((0,), (0,)), ((), ())), preferred_element_type=F32)


def contract_cols(left, right):
    return lax.dot_general(left, right, (((1,), (1,)), ((), ())), preferred_element_type=F32)


def dot(left, right):
    return jnp.dot(left, right, preferred_element_type=F32)


def call(kernel, name, scalars, ins, outs, scratch=()):
    size = sum(a.size * a.dtype.itemsize for a in ins)
    vmem, smem = pl.BlockSpec(memory_space=pltpu.VMEM), pl.BlockSpec(memory_space=pltpu.SMEM)
    return pl.pallas_call(
        kernel,
        in_specs=[smem] + [vmem] * len(ins),
        out_specs=[pl.BlockSpec(memory_space=out[2]) if len(out) > 2 else vmem for out in outs],
        out_shape=[jax.ShapeDtypeStruct(out[0], out[1]) for out in outs],
        scratch_shapes=list(scratch),
        compiler_params=PARAMS,
        cost_estimate=pl.CostEstimate(flops=2**31, bytes_accessed=size, transcendentals=0),
        name=name,
    )(scalars, *ins)


class Writer:
    def __init__(self, sems):
        self.sems, self.started = sems, []

    def write(self, source, target):
        copy = pltpu.make_async_copy(source, target, self.sems.at[len(self.started)])
        copy.start()
        self.started.append(copy)

    def finish(self):
        for copy in self.started:
            copy.wait()


def sixths(width):
    step = width // 6
    return [pl.ds(j * step, step) for j in range(6)]


def stacked(pieces, cols):
    return jnp.concatenate([p[:, cols] for p in pieces], axis=0)


OWNER_AT, PLACE_AT, FLAG_AT = 16, 17, 18
TOO_MANY = -1e30


def select_kernel(s, *refs):
    pieces, outs = refs[:4], refs[4:8]
    pick_ref, spread_ref, flag_ref = refs[8:11]
    width = pieces[0].shape[1]
    tail = jnp.concatenate([p[:, width - BLK :] for p in pieces], axis=0).astype(F32)
    lane = lax.broadcasted_iota(jnp.int32, (PLANE, BLK), 1)
    row = lax.broadcasted_iota(jnp.int32, (PLANE, BLK), 0)
    numbers = jnp.where(lane < OWNER_AT, tail, 0.0)
    needs = jnp.zeros((PLANE, BLK), F32)
    for r in range(SIDE):
        low = (s[2 + r] * 4).astype(F32)
        inside = jnp.where((numbers > low + 0.5) & (numbers < low + 4.5), 1.0, 0.0)
        needs = jnp.where(lane == r, jnp.max(inside, axis=1, keepdims=True), needs)
    needs = needs.astype(BF16)
    upto = jnp.where(row <= lane, 1.0, 0.0).astype(BF16)
    same = jnp.where(row == lane, 1.0, 0.0).astype(BF16)
    down = jnp.where(lane <= row, 1.0, 0.0).astype(BF16)
    count_rows = contract_rows(needs, upto)
    need_rows = contract_rows(needs, same)
    count_cols = dot(down, needs)
    need_cols = needs.astype(F32)
    place = lax.broadcasted_iota(jnp.int32, (CAP, BLK), 0).astype(F32) + 1.0
    for r in range(SIDE):
        hit = (count_rows[r : r + 1, :] == place) & (need_rows[r : r + 1, :] > 0.5)
        pick_ref[pl.ds(r * CAP, CAP), :] = jnp.where(hit, 1.0, 0.0).astype(BF16)
    half = lane < CAP
    place = jnp.where(half, lane, lane - CAP).astype(F32) + 1.0
    for pair in range(2):
        a, b = 2 * pair, 2 * pair + 1
        count = jnp.where(half, count_cols[:, a : a + 1], count_cols[:, b : b + 1])
        need = jnp.where(half, need_cols[:, a : a + 1], need_cols[:, b : b + 1])
        hit = (count == place) & (need > 0.5)
        spread_ref[:, pl.ds(pair * BLK, BLK)] = jnp.where(hit, 1.0, 0.0).astype(BF16)
    most = jnp.max(jnp.max(count_cols, axis=1, keepdims=True), axis=0, keepdims=True)
    flag_ref[...] = jnp.broadcast_to(jnp.where(most > CAP + 0.5, 1.0, 0.0), flag_ref.shape).astype(BF16)
    pick = pick_ref[...]
    for at in range(0, width, 1024):
        cols = pl.ds(at, min(1024, width - at))
        plane = jnp.concatenate([p[:, cols] for p in pieces], axis=0)
        chosen = dot(pick, plane).astype(BF16)
        for r in range(SIDE):
            outs[r][:, cols] = chosen[r * CAP : (r + 1) * CAP]


def select(scalars, pieces):
    width = pieces[0].shape[1]
    outs = [((CAP, width), BF16)] * 4 + [((ROWS, PLANE), BF16), ((PLANE, ROWS), BF16), ((CAP, BLK), BF16)]
    *chosen, pick, spread, flag = call(select_kernel, "select", scalars, pieces, outs)
    return chosen, pick, spread, flag


def encode_kernel(slots, s, *refs):
    pieces, w_ref, b_ref, flag_ref = refs[:4], *refs[4:7]
    codes_ref, gate_ref, acc = refs[7:10]
    width, latents = w_ref.shape[1:]
    acc[...] = jnp.broadcast_to(b_ref[...], acc.shape)
    for cols in sixths(width):
        acc[...] += dot(stacked(pieces, cols), w_ref[0, cols, :])
    lane = lax.broadcasted_iota(jnp.int32, (CAP, BLK), 1)
    for r in range(SIDE):
        rows = pl.ds(r * CAP, CAP)
        tail = pieces[r][:, pl.ds(width, BLK)]
        codes_ref[rows, pl.ds(latents, BLK)] = jnp.where(lane == FLAG_AT, flag_ref[...].astype(F32), tail.astype(F32)).astype(BF16)
        here = jnp.where(lane < slots, tail.astype(F32), 0.0)
        for b in range(latents // BLK):
            number = (s[0] * (latents // BLK) + (b + 1)).astype(F32)
            active = jnp.max(jnp.where(here == number, 1.0, 0.0), axis=1, keepdims=True)
            pre = acc[rows, pl.ds(b * BLK, BLK)]
            decay = jnp.exp(-jnp.abs(pre))
            soft = jnp.maximum(pre, 0.0) + jnp.log1p(decay)
            slope = jnp.where(pre >= 0, 1.0, decay) / (1.0 + decay)
            codes_ref[rows, pl.ds(b * BLK, BLK)] = (active * soft).astype(BF16)
            gate_ref[rows, pl.ds(b * BLK, BLK)] = active * slope


def encode(scalars, pieces, w_enc, b_enc, flag, slots):
    latents = w_enc.shape[2]
    outs = [((ROWS, latents + BLK), BF16), ((ROWS, latents), F32)]
    kernel = functools.partial(encode_kernel, slots)
    return call(kernel, "encode", scalars, [*pieces, w_enc, b_enc, flag], outs, [pltpu.VMEM((ROWS, latents), F32)])


def decode_self_kernel(slots, s, codes_ref, w_ref, sum_ref, slot_ref):
    latents, width = w_ref.shape[1:]
    for cols in sixths(width):
        sum_ref[:, cols] = dot(codes_ref[:, pl.ds(0, latents)], w_ref[0, :, cols])
    lane = lax.broadcasted_iota(jnp.int32, (CAP, BLK), 1)
    for r in range(SIDE):
        rows = pl.ds(r * CAP, CAP)
        here = jnp.where(lane < slots, codes_ref[rows, pl.ds(latents, BLK)].astype(F32), 0.0)
        picked = [jnp.zeros((CAP, BLK), F32) for _ in range(slots)]
        for b in range(latents // BLK):
            number = (s[0] * (latents // BLK) + (b + 1)).astype(F32)
            wide = codes_ref[rows, pl.ds(b * BLK, BLK)].astype(F32)
            for k in range(slots):
                picked[k] = jnp.where(here[:, k : k + 1] == number, wide, picked[k])
        for k in range(slots):
            slot_ref[rows, pl.ds(k * BLK, BLK)] = picked[k].astype(BF16)


def decode_self(scalars, codes, w_self, slots):
    outs = [((ROWS, w_self.shape[2]), F32), ((ROWS, slots * BLK), BF16)]
    return call(functools.partial(decode_self_kernel, slots), "decode_self", scalars, [codes, w_self], outs)


def decode_kernel(s, own_ref, other_ref, sum_ref, cross_first_ref, cross_ref, slot_ref, *refs):
    outs, source_ref, match_ref = refs[:4], refs[4], refs[5]
    latents, half = cross_ref.shape
    width = 2 * half
    first = s[1] == 0
    own, other = own_ref[:, pl.ds(latents, BLK)], other_ref[:, pl.ds(latents, BLK)]
    one, zero = jnp.where(first, other, own), jnp.where(first, own, other)
    lane = lax.broadcasted_iota(jnp.int32, (8, BLK), 1)
    row = lax.broadcasted_iota(jnp.int32, (8, BLK), 0)
    take = jnp.where(lane == row + OWNER_AT, 1.0, 0.0).astype(BF16)

    def matched(cols, rows):
        numbers = contract_cols(take, rows)
        owner = cols[:, OWNER_AT : OWNER_AT + 1].astype(F32)
        place = cols[:, PLACE_AT : PLACE_AT + 1].astype(F32)
        hit = (owner == numbers[0:1]) & (place == numbers[1:2]) & (owner > 0.5)
        return jnp.where(hit, 1.0, 0.0).astype(BF16)

    match_ref[...] = matched(zero, one)
    codes = jnp.where(first, own_ref[:, pl.ds(0, latents)], other_ref[:, pl.ds(0, latents)])
    source_ref[...] = dot(matched(one, zero), codes).astype(BF16)
    slots = slot_ref.shape[1]
    flag = (own + other).astype(F32)[:CAP, FLAG_AT : FLAG_AT + 1]
    flag = jnp.broadcast_to(flag, (CAP, slots)) > 0.5
    for r in range(SIDE):
        slotted = jnp.where(flag, TOO_MANY, slot_ref[pl.ds(r * CAP, CAP), :].astype(F32))
        outs[r][:, pl.ds(width, slots)] = slotted.astype(BF16)

    def put(cols, value):
        value = value.astype(BF16)
        for r in range(SIDE):
            outs[r][:, cols] = value[r * CAP : (r + 1) * CAP]

    @pl.when(first)
    def _():
        for cols in sixths(width):
            put(cols, sum_ref[:, cols])

    @pl.when(jnp.logical_not(first))
    def _():
        for cols in sixths(width):
            cross = cross_first_ref[:, cols] if cols.start < half else cross_ref[:, pl.ds(cols.start - half, cols.size)]
            put(cols, sum_ref[:, cols] + dot(source_ref[...], cross))


def decode(scalars, own, other, self_sum, w_cross_first, w_cross, slotted):
    latents, half = w_cross.shape
    wide = 2 * half + slotted.shape[1]
    outs = [((CAP, wide), BF16)] * 4 + [((ROWS, latents), BF16), ((ROWS, ROWS), BF16)]
    ins = [own, other, self_sum, w_cross_first, w_cross, slotted]
    *sums, source, match = call(decode_kernel, "decode", scalars, ins, outs)
    return sums, source, match


def spread_kernel(main, s, spread_ref, *refs):
    pieces, outs = refs[:4], refs[4:]
    width = pieces[0].shape[1]
    step = 9 * BLK
    for at in range(0, width, step):
        cols = pl.ds(at, min(step, width - at))
        total = dot(spread_ref[...], stacked(pieces, cols)).astype(BF16)
        for m in range(SIDE):
            outs[m][:, cols] = total[m * LINE : (m + 1) * LINE]
    least = jnp.min(sum(p[0:16, pl.ds(main, BLK)].astype(F32) for p in pieces))

    @pl.when(least < -0.5)
    def _():
        for m in range(SIDE):
            outs[m][:, pl.ds(main, width - main)] = jnp.full((LINE, width - main), TOO_MANY, F32).astype(BF16)


def spread_sum(scalars, spread, pieces, main):
    outs = [((LINE, pieces[0].shape[1]), BF16)] * 4
    return call(functools.partial(spread_kernel, main), "spread", scalars, [spread, *pieces], outs)


def line_kernel(s, *refs):
    pieces, targets_ref, exact_ref, sents = refs[:4], refs[4], refs[5], refs[6:]
    tokens, width = targets_ref.shape[1:]
    for cols in sixths(width):
        total = sum(p[:, cols].astype(F32) for p in pieces)
        own = total[:tokens] - targets_ref[0, :, cols].astype(F32)
        total = jnp.concatenate([own, total[tokens:]], axis=0)
        exact_ref[:, cols] = total
        for sent in sents:
            sent[:, cols] = total.astype(BF16)
    slots = exact_ref.shape[1] - width
    quarter = slots // SIDE
    total = sum(p[:, pl.ds(width, slots)].astype(F32) for p in pieces)
    exact_ref[:, pl.ds(width, slots)] = total
    for r in (1, 2, 3):
        i = AWAY.index(-AWAY[r] % SIDE)
        rows = total[tokens * i : tokens * (i + 1)]
        folded = jnp.concatenate([rows[:, quarter * c : quarter * (c + 1)] for c in range(SIDE)], axis=0)
        sents[r - 1][:, pl.ds(width, quarter)] = folded.astype(BF16)


def line_terms(scalars, pieces, targets):
    rows, columns = pieces[0].shape
    width = targets.shape[2]
    outs = [((rows, columns), F32)] + [((rows, width + (columns - width) // SIDE), BF16)] * 3
    exact, *sents = call(line_kernel, "line", scalars, [*pieces, targets], outs)
    return exact, [exact, *sents]


def settle_kernel(s, exact_ref, *refs):
    came, targets_ref, err_ref, recon_ref, tail_ref = refs[:3], *refs[3:]
    tokens, width = targets_ref.shape[1:]
    for cols in sixths(width):
        total = exact_ref[:, cols]
        for r in (1, 2, 3):
            value = came[r - 1][:, cols].astype(F32)
            order = [AWAY.index((AWAY[j] - AWAY[r]) % SIDE) for j in range(SIDE)]
            total += jnp.concatenate([value[tokens * i : tokens * (i + 1)] for i in order], axis=0)
        err_ref[:, cols] = total.astype(BF16)
        recon_ref[0, :, cols] = total[:tokens] + targets_ref[0, :, cols].astype(F32)
    slots = tail_ref.shape[1]
    tail = exact_ref[0:tokens, pl.ds(width, slots)]
    for r in (1, 2, 3):
        value = came[r - 1][:, pl.ds(width, slots // SIDE)].astype(F32)
        tail += jnp.concatenate([value[tokens * c : tokens * (c + 1)] for c in range(SIDE)], axis=1)
    tail_ref[...] = tail


def settle(scalars, exact, came, targets):
    rows, columns = exact.shape
    tokens, width = targets.shape[1:]
    outs = [((rows, width), BF16), ((1, tokens, width), F32), ((tokens, columns - width), F32)]
    return call(settle_kernel, "settle", scalars, [exact, *came, targets], outs)


def compact_kernel(s, pick_ref, *refs):
    pieces, outs = refs[:4], refs[4:]
    for cols in sixths(pieces[0].shape[1]):
        chosen = dot(pick_ref[...], stacked(pieces, cols)).astype(BF16)
        for r in range(SIDE):
            outs[r][:, cols] = chosen[r * CAP : (r + 1) * CAP]


def compact(scalars, pick, pieces):
    outs = [((CAP, pieces[0].shape[1]), BF16)] * 4
    return call(compact_kernel, "compact", scalars, [pick, *pieces], outs)


def cross_kernel(s, match_ref, cross_first_ref, cross_ref, *refs):
    pieces, out_ref, acc = refs[:4], refs[4], refs[5]
    latents, half = cross_ref.shape

    @pl.when(s[1] != 0)
    def _():
        acc[...] = jnp.zeros(acc.shape, F32)
        for cols in sixths(2 * half):
            err = stacked(pieces, cols)
            if cols.start < half:
                out_ref[:, cols] = err
                acc[...] += contract_cols(err, cross_first_ref[:, cols])
            else:
                acc[...] += contract_cols(err, cross_ref[:, pl.ds(cols.start - half, cols.size)])
        value = acc[...]
        high = value.astype(BF16)
        rest = (value - high.astype(F32)).astype(BF16)
        turned = dot(match_ref[...], high) + dot(match_ref[...], rest)
        high = turned.astype(BF16)
        out_ref[:, pl.ds(half, latents)] = high
        out_ref[:, pl.ds(half + latents, latents)] = (turned - high.astype(F32)).astype(BF16)


def cross_back(scalars, match, pieces, w_cross_first, w_cross):
    latents, half = w_cross.shape
    outs = [((ROWS, half + 2 * latents), BF16)]
    ins = [match, w_cross_first, w_cross, *pieces]
    return call(cross_kernel, "cross_back", scalars, ins, outs, [pltpu.VMEM((ROWS, latents), F32)])[0]


def self_kernel(s, codes_ref, w_ref, *refs):
    pieces, term_ref, grad_ref, turned, grad, sems = refs[:4], *refs[4:]
    latents, width = w_ref.shape[1:]
    writer = Writer(sems)
    turned[...] = codes_ref[:, pl.ds(0, latents)].T
    term_ref[...] = jnp.zeros(term_ref.shape, F32)
    for cols in sixths(width):
        err = stacked(pieces, cols)
        grad[:, cols] = dot(turned[...], err).astype(BF16)
        writer.write(grad.at[:, cols], grad_ref.at[0, :, cols])
        term_ref[...] += contract_cols(err, w_ref[0, :, cols])
    writer.finish()


def self_back(scalars, codes, pieces, w_self):
    latents, width = w_self.shape[1:]
    outs = [((ROWS, latents), F32), (w_self.shape, BF16, pltpu.HBM)]
    scratch = [pltpu.VMEM((latents, ROWS), BF16), pltpu.VMEM((latents, width), BF16), pltpu.SemaphoreType.DMA((6,))]
    return call(self_kernel, "self_back", scalars, [codes, w_self, *pieces], outs, scratch)


def last_kernel(s, term_ref, gate_ref, source_ref, returned_ref, tail_ref, *refs):
    x, errs = refs[:4], refs[4:8]
    enc_ref, bias_ref, cross_ref, picked_ref, again_ref = refs[8:13]
    dpre, turned, enc, cross, sems = refs[13:]
    width, half = enc.shape[0], cross.shape[1]
    writer = Writer(sems)
    latents = dpre.shape[1]
    again_ref[0] = jnp.where(jnp.min(tail_ref[...]) < -0.5, 1, 0)
    back = [returned_ref[:, pl.ds(at, latents)].astype(F32) for at in (half, half + latents)]
    value = ((term_ref[...] + (back[0] + back[1])) * gate_ref[...]).astype(BF16)
    dpre[...] = value
    bias_ref[...] = jnp.sum(value.astype(F32), axis=0, keepdims=True)
    for cols in sixths(width):
        enc[cols, :] = contract_rows(stacked(x, cols), dpre[...]).astype(BF16)
        writer.write(enc.at[cols, :], enc_ref.at[0, cols, :])
    tokens, slots = tail_ref.shape[0], tail_ref.shape[1] // BLK
    rows = [tail_ref[t : t + 1, pl.ds(k * BLK, BLK)] for t in range(tokens) for k in range(slots)]
    picked_ref[...] = jnp.concatenate(rows, axis=0).astype(BF16)
    turned[...] = source_ref[...].T
    step = half // 3
    for j in range(3):
        cols = pl.ds(j * step, step)

        @pl.when(s[1] == 0)
        def _():
            cross[:, cols] = dot(turned[...], returned_ref[:, cols]).astype(BF16)

        @pl.when(s[1] != 0)
        def _():
            err = stacked(errs, pl.ds(half + cols.start, step))
            cross[:, cols] = dot(turned[...], err).astype(BF16)

        writer.write(cross.at[:, cols], cross_ref.at[:, cols])
    writer.finish()


def last(scalars, term, gate, source, returned, tail, x, errs):
    latents, half = source.shape[1], returned.shape[1] - 2 * source.shape[1]
    picked = tail.shape[0] * tail.shape[1] // BLK
    outs = [((1, 2 * half, latents), BF16, pltpu.HBM), ((1, latents), F32), ((latents, half), BF16, pltpu.HBM)]
    outs += [((picked, BLK), BF16), ((1,), jnp.int32, pltpu.SMEM)]
    scratch = [pltpu.VMEM((ROWS, latents), BF16), pltpu.VMEM((latents, ROWS), BF16)]
    scratch += [pltpu.VMEM((2 * half, latents), BF16), pltpu.VMEM((latents, half), BF16)]
    scratch += [pltpu.SemaphoreType.DMA((9,))]
    ins = [term, gate, source, returned, tail, *x, *errs]
    return call(last_kernel, "last", scalars, ins, outs, scratch)


def reorder(rows, axes):
    shape = (SIDE, SIDE, SIDE, -1, rows.shape[-1])
    return jnp.transpose(rows.reshape(shape), (*axes, 3, 4)).reshape(rows.shape)


def to_second_order(rows):
    return reorder(rows, (2, 0, 1))


def to_first_order(rows):
    return reorder(rows, (1, 2, 0))


def gather_all(rows):
    for axes in (INNER, MIDDLE, OUTER):
        rows = jnp.concatenate(line_gather(rows, axes), axis=0)
    return rows


def reduce_all(rows):
    for axes in (OUTER, MIDDLE, INNER):
        rows = line_reduce(jnp.split(rows, SIDE, axis=0), axes)
    return rows


def dense(inputs, targets, w_enc, b_enc, w_self, w_cross, block_ids, w_cross_first):
    first_layer = lax.axis_index("layer") == 0
    width = inputs.shape[2]
    half = width // 2
    blocks = w_enc.shape[2] // BLK
    slots = block_ids.shape[2]
    tail = jnp.pad(block_ids[0].astype(BF16), ((0, 0), (0, BLK - slots)))
    gathered = gather_all(jnp.concatenate([inputs[0], tail], axis=1))
    x, ids = gathered[:, :width], gathered[:, width : width + slots].astype(jnp.int32)
    own_blocks = lax.axis_index("feat") * blocks + jnp.arange(blocks, dtype=jnp.int32)
    hit = ids[:, :, None] == own_blocks[None, None, :]
    active = jnp.repeat(jnp.any(hit, axis=1), BLK, axis=1).astype(F32)
    pre = dot(x, w_enc[0]) + b_enc[0]
    codes = (active * jax.nn.softplus(pre)).astype(BF16)
    turned = to_second_order(codes)
    earlier = to_second(turned)
    source = jnp.where(first_layer, turned, earlier)
    by_block = codes.reshape(-1, 1, blocks, BLK)
    slotted = jnp.sum(jnp.where(hit[..., None], by_block, 0).astype(F32), axis=2).reshape(-1, slots * BLK)
    w_cross_all = jnp.concatenate([w_cross_first, w_cross], axis=1)
    partial = dot(codes, w_self[0]) + dot(earlier, w_cross_all)
    summed = reduce_all(jnp.concatenate([partial, slotted], axis=1).astype(BF16))
    recon = summed[:, :width]
    picked = summed[:, width:].astype(BF16).reshape(-1, slots, BLK)
    err = gather_all((recon - targets[0].astype(F32)).astype(BF16))
    back = to_first_order(to_first(contract_cols(err, w_cross_all)))
    returned = to_first(err[:, :half])
    term = contract_cols(err, w_self[0])
    grad_self = contract_rows(codes, err).astype(BF16)
    cross_err = jnp.where(first_layer, returned, err[:, half:])
    grad_cross = contract_rows(source, cross_err).astype(BF16)
    code_grads = term + jnp.where(first_layer, back, 0.0)
    pre_grads = (code_grads * active * jax.nn.sigmoid(pre)).astype(BF16)
    grad_enc = contract_rows(x, pre_grads).astype(BF16)
    grad_benc = jnp.sum(pre_grads.astype(F32), axis=0)
    return recon, picked, grad_enc, grad_benc[None], grad_self, grad_cross


def per_device(inputs, targets, w_enc, b_enc, w_self, w_cross, block_ids):
    layer = lax.axis_index("layer")
    shard = lax.axis_index("feat")
    width = inputs.shape[2]
    slots = block_ids.shape[2]
    tokens_dev = inputs.shape[1]

    y, z = shard // (SIDE * SIDE), shard % SIDE
    receivers = [
        jnp.where(layer == 0, shard - z + (z - r) % SIDE, shard + SIDE * SIDE * ((y - r) % SIDE - y))
        for r in AWAY
    ]
    scalars = jnp.stack([shard, layer] + receivers).astype(jnp.int32)

    own_ids, other_ids = (ids[0].astype(BF16) + 1 for ids in (block_ids, swapped(block_ids)))
    owner = jnp.full((tokens_dev, 1), shard + 1).astype(BF16)
    place = jnp.arange(tokens_dev, dtype=jnp.int32)[:, None].astype(BF16)
    spare = jnp.zeros((tokens_dev, BLK - 2 * slots - 2), BF16)
    rows = jnp.concatenate([inputs[0], own_ids, other_ids, owner, place, spare], axis=1)

    line = jnp.concatenate(line_gather(rows, INNER), axis=0)
    chosen, pick, spread, flag = select(scalars, line_gather(line, MIDDLE))
    x = ahead(chosen[0], chosen, OUTER)
    x, half_cross = lax.optimization_barrier((x, w_cross))
    w_cross_first = to_second(half_cross)
    codes, gate = encode(scalars, x, w_enc, b_enc, flag, slots)
    other_codes = swapped(codes)
    self_sum, slotted = decode_self(scalars, codes, w_self, slots)
    sums, source, match = decode(scalars, codes, other_codes, self_sum, w_cross_first, w_cross, slotted)
    sums = behind(sums, OUTER)
    exact, sents = line_terms(scalars, behind(spread_sum(scalars, spread, sums, width), MIDDLE), targets)
    err_line, recon, tail = settle(scalars, exact, ahead(exact, sents, INNER)[1:], targets)
    err_plane = line_gather(err_line, MIDDLE)
    kept = compact(scalars, pick, err_plane)
    errs = ahead(kept[0], kept, OUTER)
    returned = to_first(cross_back(scalars, match, errs, w_cross_first, w_cross))
    term, grad_self = self_back(scalars, codes, errs, w_self)
    grad_enc, grad_benc, grad_cross, picked, again = last(scalars, term, gate, source, returned, tail, x, errs)

    def on_every_row(_):
        results = dense(inputs, targets, w_enc, b_enc, w_self, w_cross, block_ids, w_cross_first)
        recon, picked, grad_enc, grad_benc, grad_self, grad_cross = results
        return jnp.int32(0), recon[None], picked.reshape(-1, BLK), grad_enc[None], grad_benc, grad_self[None], grad_cross

    results = (again[0], recon, picked, grad_enc, grad_benc, grad_self, grad_cross)
    _, recon, picked, *grads = lax.while_loop(lambda carried: carried[0] > 0, on_every_row, results)
    return recon, picked.reshape(1, tokens_dev, slots, BLK), *grads


def solution(mesh):
    placed = (
        P("layer", "feat", None),
        P("layer", "feat", None),
        P("layer", None, "feat"),
        P("layer", "feat"),
        P("layer", "feat", None),
        P("feat", "layer"),
        P("layer", "feat", None),
    )
    return jax.shard_map(
        per_device,
        mesh=mesh,
        in_specs=placed,
        out_specs=(
            P("layer", "feat", None),
            P("layer", "feat", None, None),
            P("layer", None, "feat"),
            P("layer", "feat"),
            P("layer", "feat", None),
            P("feat", "layer"),
        ),
        check_vma=False,
    )
```

profile of v0, /device:TPU:1, one launch (start us, length us, event | category | flops | bytes accessed | tf_op | source)
XLA Modules:
  0.0 146.6 jit_solution(13730446823192676454)
XLA Ops:
  0.6 1.5 %collective-permute-start.30 = (s32[1,8,8]{2,1,0:T(8,128)}, s32[1,8,8]{2,1,0:T(8,128)S(1)}, u32[]{:S(2)}, u32[]{:S(2)}) collective-permute-start(s32[1,8,8]{2,1,0:T(8,128)} %param.15), channel_id=1, source_target_pairs={{0,64},{64,0},{1,65},{65,1},{2,66},{66,2},{3,67},{67,3},{4,68},{68... | collective-permute-start | bytes 776 | tf_op jit(solution)/shard_map/ppermute | solution.py:63
  3.2 1.0 concatenate.38
  4.2 2.8 %collective-permute-start.31 = (bf16[8,4736]{1,0:T(8,128)(2,1)S(1)}, bf16[8,4736]{1,0:T(8,128)(2,1)S(1)}, u32[]{:S(2)}, u32[]{:S(2)}) collective-permute-start(bf16[8,4736]{1,0:T(8,128)(2,1)S(1)} %concatenate.38), channel_id=1, source_target_pairs={{0,32},{1,33},{2,34},{3,35},{4,36},{5,37},{6,38},{7,39},{8,40},{9,... | collective-permute-start | bytes 227336 | tf_op jit(solution)/shard_map/ppermute | solution.py:43
  7.0 0.9 collective-permute-start.32
  9.2 1.0 collective-permute-done.32
  10.2 2.1 %collective-permute-done.33 = bf16[8,4736]{1,0:T(8,128)(2,1)S(1)} collective-permute-done((bf16[8,4736]{1,0:T(8,128)(2,1)S(1)}, bf16[8,4736]{1,0:T(8,128)(2,1)S(1)}, u32[]{:S(2)}, u32[]{:S(2)}) %collective-permute-start.33) | collective-permute-done | bytes 75808 | tf_op jit(solution)/shard_map/ppermute | solution.py:43
  12.3 3.7 %collective-permute-start.34 = (bf16[32,4736]{1,0:T(8,128)(2,1)S(1)}, bf16[32,4736]{1,0:T(8,128)(2,1)S(1)}, u32[]{:S(2)}, u32[]{:S(2)}) collective-permute-start(bf16[32,4736]{1,0:T(8,128)(2,1)S(1)} %pad_maximum_fusion.4.refs_0_), channel_id=1, source_target_pairs={{0,8},{1,9},{2,10},{3,11},{4,12},{5,13},{6,14},{7,15},{8,0},{9,1},... | collective-permute-start | bytes 909320 | tf_op jit(solution)/shard_map/ppermute | solution.py:43
  16.4 1.0 collective-permute-start.36
  17.6 2.9 %collective-permute-done.34.refs_1_ = bf16[32,4736]{1,0:T(8,128)(2,1)S(1)} collective-permute-done((bf16[32,4736]{1,0:T(8,128)(2,1)S(1)}, bf16[32,4736]{1,0:T(8,128)(2,1)S(1)}, u32[]{:S(2)}, u32[]{:S(2)}) %collective-permute-start.34) | collective-permute-done | bytes 303136 | tf_op jit(solution)/shard_map/ppermute | solution.py:43
  20.5 4.0 %collective-permute-done.35.refs_2_ = bf16[32,4736]{1,0:T(8,128)(2,1)S(1)} collective-permute-done((bf16[32,4736]{1,0:T(8,128)(2,1)S(1)}, bf16[32,4736]{1,0:T(8,128)(2,1)S(1)}, u32[]{:S(2)}, u32[]{:S(2)}) %collective-permute-start.35) | collective-permute-done | bytes 303136 | tf_op jit(solution)/shard_map/ppermute | solution.py:43
  24.5 1.7 %select.26 = (bf16[64,4736]{1,0:T(8,128)(2,1)S(1)}, bf16[64,4736]{1,0:T(8,128)(2,1)S(1)}, bf16[64,4736]{1,0:T(8,128)(2,1)S(1)}, bf16[64,4736]{1,0:T(8,128)(2,1)S...) custom-call(s32[6]{0:T(128)S(1)} %stack.27.s, ...), custom_call_target="tpu_custom_call" | custom-call | flops 2147483648 | bytes 1212416 | tf_op jit(solution)/shard_map/select/pallas_call | solution.py:90
  26.2 2.7 %collective-permute-start.37 = (bf16[64,4736]{1,0:T(8,128)(2,1)S(1)}, bf16[64,4736]{1,0:T(8,128)(2,1)S(1)}, u32[]{:S(2)}, u32[]{:S(2)}) collective-permute-start(bf16[64,4736]{1,0:T(8,128)(2,1)S(1)} %get-tuple-element.126), channel_id=1, source_target_pairs={{0,2},{1,3},{2,0},{3,1},{4,6},{5,7},{6,4},{7,5},{8,10},{9,11},{10,... | collective-permute-start | bytes 1818632 | tf_op jit(solution)/shard_map/ppermute | solution.py:43
  28.9 1.1 collective-permute-start.38
  30.4 6.7 %collective-permute-done.37.refs_1_ = bf16[64,4736]{1,0:T(8,128)(2,1)S(1)} collective-permute-done((bf16[64,4736]{1,0:T(8,128)(2,1)S(1)}, bf16[64,4736]{1,0:T(8,128)(2,1)S(1)}, u32[]{:S(2)}, u32[]{:S(2)}) %collective-permute-start.37) | collective-permute-done | bytes 606240 | tf_op jit(solution)/shard_map/ppermute | solution.py:43
  37.1 6.5 %collective-permute-done.38.refs_2_ = bf16[64,4736]{1,0:T(8,128)(2,1)S(1)} collective-permute-done((bf16[64,4736]{1,0:T(8,128)(2,1)S(1)}, bf16[64,4736]{1,0:T(8,128)(2,1)S(1)}, u32[]{:S(2)}, u32[]{:S(2)}) %collective-permute-start.38) | collective-permute-done | bytes 606240 | tf_op jit(solution)/shard_map/ppermute | solution.py:43
  43.6 1.3 collective-permute-start.41
  44.9 2.3 %encode.1 = (bf16[256,640]{1,0:T(8,128)(2,1)S(1)}, f32[256,512]{1,0:T(8,128)S(1)}) custom-call(s32[6]{0:T(128)S(1)} %stack.27.s, bf16[64,4736]{1,0:T(8,128)(2,1)S(1)} %get-tuple-element.129.refs_0_, bf16[64,4736]{1,0:T(8,128)(2,1)S(1)} %collective-permute-done.37.refs_1_, bf16[64,4736]{1,0:T(8,128)(2,1)S(1)} %collective-permute-done.38.refs_2_, ...), custom_call_target="tpu_custom_call" | custom-call | flops 2147483648 | bytes 7161856 | tf_op jit(solution)/shard_map/encode/pallas_call | solution.py:90
  47.2 4.6 %collective-permute-start.40 = (bf16[256,640]{1,0:T(8,128)(2,1)S(1)}, bf16[256,640]{1,0:T(8,128)(2,1)S(1)}, u32[]{:S(2)}, u32[]{:S(2)}) collective-permute-start(bf16[256,640]{1,0:T(8,128)(2,1)S(1)} %get-tuple-element.134.codes_ref.own_ref), channel_id=1, source_target_pairs={{0,64},{64,0},{1,65},{65,1},{2,66},{66,2},{3,67},{67,3},{4,68},{68... | collective-permute-start | bytes 983048 | tf_op jit(solution)/shard_map/ppermute | solution.py:63
  51.8 2.0 %decode_self.1 = (f32[256,4608]{1,0:T(8,128)S(1)}, bf16[256,1024]{1,0:T(8,128)(2,1)S(1)}) custom-call(s32[6]{0:T(128)S(1)} %stack.27.s, bf16[256,640]{1,0:T(8,128)(2,1)S(1)} %get-tuple-element.134.codes_ref.own_ref, bf16[1,512,4608]{2,1,0:T(8,128)(2,1)S(1)} %bitcast.81), custom_call_target="tpu_custom_call" | custom-call | flops 2147483648 | bytes 5046272 | tf_op jit(solution)/shard_map/decode_self/pallas_call | solution.py:90
  53.8 2.4 %decode.1 = (bf16[64,5632]{1,0:T(8,128)(2,1)S(1)}, bf16[64,5632]{1,0:T(8,128)(2,1)S(1)}, bf16[64,5632]{1,0:T(8,128)(2,1)S(1)}, bf16[64,5632]{1,0:T(8,128)(2,1)S(...) custom-call(s32[6]{0:T(128)S(1)} %stack.27.s, bf16[256,640]{1,0:T(8,128)(2,1)S(1)} %get-tuple-element.134.codes_ref.own_ref, ...), custom_call_target="tpu_custom_call" | custom-call | flops 2147483648 | bytes 10616832 | tf_op jit(solution)/shard_map/decode/pallas_call | solution.py:90
  56.6 2.6 %collective-permute-start.44 = (bf16[64,5632]{1,0:T(8,128)(2,1)S(1)}, bf16[64,5632]{1,0:T(8,128)(2,1)S(1)}, u32[]{:S(2)}, u32[]{:S(2)}) collective-permute-start(bf16[64,5632]{1,0:T(8,128)(2,1)S(1)} %get-tuple-element.143), channel_id=1, source_target_pairs={{0,3},{1,0},{2,1},{3,2},{4,7},{5,4},{6,5},{7,6},{8,11},{9,8},{10,9... | collective-permute-start | bytes 2162696 | tf_op jit(solution)/shard_map/ppermute | solution.py:43
  59.2 8.9 %collective-permute-done.42.refs_1_ = bf16[64,5632]{1,0:T(8,128)(2,1)S(1)} collective-permute-done((bf16[64,5632]{1,0:T(8,128)(2,1)S(1)}, bf16[64,5632]{1,0:T(8,128)(2,1)S(1)}, u32[]{:S(2)}, u32[]{:S(2)}) %collective-permute-start.42) | collective-permute-done | bytes 720928 | tf_op jit(solution)/shard_map/ppermute | solution.py:43
  68.0 7.5 %collective-permute-done.43.refs_2_ = bf16[64,5632]{1,0:T(8,128)(2,1)S(1)} collective-permute-done((bf16[64,5632]{1,0:T(8,128)(2,1)S(1)}, bf16[64,5632]{1,0:T(8,128)(2,1)S(1)}, u32[]{:S(2)}, u32[]{:S(2)}) %collective-permute-start.43) | collective-permute-done | bytes 720928 | tf_op jit(solution)/shard_map/ppermute | solution.py:43
  75.6 1.1 spread.1
  76.7 2.3 %collective-permute-start.45 = (bf16[32,5632]{1,0:T(8,128)(2,1)S(1)}, bf16[32,5632]{1,0:T(8,128)(2,1)S(1)}, u32[]{:S(2)}, u32[]{:S(2)}) collective-permute-start(bf16[32,5632]{1,0:T(8,128)(2,1)S(1)} %get-tuple-element.145), channel_id=1, source_target_pairs={{0,8},{1,9},{2,10},{3,11},{4,12},{5,13},{6,14},{7,15},{8,0},{9,1},... | collective-permute-start | bytes 1081352 | tf_op jit(solution)/shard_map/ppermute | solution.py:43
  79.0 0.7 collective-permute-start.46
  79.7 1.9 %collective-permute-start.47 = (bf16[32,5632]{1,0:T(8,128)(2,1)S(1)}, bf16[32,5632]{1,0:T(8,128)(2,1)S(1)}, u32[]{:S(2)}, u32[]{:S(2)}) collective-permute-start(bf16[32,5632]{1,0:T(8,128)(2,1)S(1)} %get-tuple-element.147), channel_id=1, source_target_pairs={{0,12},{1,13},{2,14},{3,15},{4,0},{5,1},{6,2},{7,3},{8,4},{9,5},{1... | collective-permute-start | bytes 1081352 | tf_op jit(solution)/shard_map/ppermute | solution.py:43
  81.6 3.3 %collective-permute-done.45.refs_1_ = bf16[32,5632]{1,0:T(8,128)(2,1)S(1)} collective-permute-done((bf16[32,5632]{1,0:T(8,128)(2,1)S(1)}, bf16[32,5632]{1,0:T(8,128)(2,1)S(1)}, u32[]{:S(2)}, u32[]{:S(2)}) %collective-permute-start.45) | collective-permute-done | bytes 360480 | tf_op jit(solution)/shard_map/ppermute | solution.py:43
  84.9 3.8 %collective-permute-done.46.refs_2_ = bf16[32,5632]{1,0:T(8,128)(2,1)S(1)} collective-permute-done((bf16[32,5632]{1,0:T(8,128)(2,1)S(1)}, bf16[32,5632]{1,0:T(8,128)(2,1)S(1)}, u32[]{:S(2)}, u32[]{:S(2)}) %collective-permute-start.46) | collective-permute-done | bytes 360480 | tf_op jit(solution)/shard_map/ppermute | solution.py:43
  89.5 2.2 %collective-permute-start.48 = (bf16[32,4864]{1,0:T(8,128)(2,1)S(1)}, bf16[32,4864]{1,0:T(8,128)(2,1)S(1)}, u32[]{:S(2)}, u32[]{:S(2)}) collective-permute-start(bf16[32,4864]{1,0:T(8,128)(2,1)S(1)} %get-tuple-element.149), channel_id=1, source_target_pairs={{0,32},{1,33},{2,34},{3,35},{4,36},{5,37},{6,38},{7,39},{8,40},{9,... | collective-permute-start | bytes 933896 | tf_op jit(solution)/shard_map/ppermute | solution.py:43
  91.6 0.9 collective-permute-start.49
  93.1 4.0 %collective-permute-done.48.refs_0_ = bf16[32,4864]{1,0:T(8,128)(2,1)S(1)} collective-permute-done((bf16[32,4864]{1,0:T(8,128)(2,1)S(1)}, bf16[32,4864]{1,0:T(8,128)(2,1)S(1)}, u32[]{:S(2)}, u32[]{:S(2)}) %collective-permute-start.48) | collective-permute-done | bytes 311328 | tf_op jit(solution)/shard_map/ppermute | solution.py:43
  97.1 2.8 %collective-permute-done.49.refs_1_ = bf16[32,4864]{1,0:T(8,128)(2,1)S(1)} collective-permute-done((bf16[32,4864]{1,0:T(8,128)(2,1)S(1)}, bf16[32,4864]{1,0:T(8,128)(2,1)S(1)}, u32[]{:S(2)}, u32[]{:S(2)}) %collective-permute-start.49) | collective-permute-done | bytes 311328 | tf_op jit(solution)/shard_map/ppermute | solution.py:43
  100.4 1.2 settle.1
  101.7 1.7 %collective-permute-start.51 = (bf16[32,4608]{1,0:T(8,128)(2,1)S(1)}, bf16[32,4608]{1,0:T(8,128)(2,1)S(1)}, u32[]{:S(2)}, u32[]{:S(2)}) collective-permute-start(bf16[32,4608]{1,0:T(8,128)(2,1)S(1)} %get-tuple-element.152.refs_0_), channel_id=1, source_target_pairs={{0,8},{1,9},{2,10},{3,11},{4,12},{5,13},{6,14},{7,15},{8,0},{9,1},... | collective-permute-start | bytes 884744 | tf_op jit(solution)/shard_map/ppermute | solution.py:43
  103.4 1.4 collective-permute-start.52
  104.9 4.2 %collective-permute-done.51.refs_1_ = bf16[32,4608]{1,0:T(8,128)(2,1)S(1)} collective-permute-done((bf16[32,4608]{1,0:T(8,128)(2,1)S(1)}, bf16[32,4608]{1,0:T(8,128)(2,1)S(1)}, u32[]{:S(2)}, u32[]{:S(2)}) %collective-permute-start.51) | collective-permute-done | bytes 294944 | tf_op jit(solution)/shard_map/ppermute | solution.py:43
  109.0 3.2 %collective-permute-done.52.refs_2_ = bf16[32,4608]{1,0:T(8,128)(2,1)S(1)} collective-permute-done((bf16[32,4608]{1,0:T(8,128)(2,1)S(1)}, bf16[32,4608]{1,0:T(8,128)(2,1)S(1)}, u32[]{:S(2)}, u32[]{:S(2)}) %collective-permute-start.52) | collective-permute-done | bytes 294944 | tf_op jit(solution)/shard_map/ppermute | solution.py:43
  112.2 1.3 compact.1
  113.6 1.7 %collective-permute-start.55 = (bf16[64,4608]{1,0:T(8,128)(2,1)S(1)}, bf16[64,4608]{1,0:T(8,128)(2,1)S(1)}, u32[]{:S(2)}, u32[]{:S(2)}) collective-permute-start(bf16[64,4608]{1,0:T(8,128)(2,1)S(1)} %get-tuple-element.155), channel_id=1, source_target_pairs={{0,3},{1,0},{2,1},{3,2},{4,7},{5,4},{6,5},{7,6},{8,11},{9,8},{10,9... | collective-permute-start | bytes 1769480 | tf_op jit(solution)/shard_map/ppermute | solution.py:43
  115.3 8.9 %collective-permute-done.54.refs_1_.refs_5_ = bf16[64,4608]{1,0:T(8,128)(2,1)S(1)} collective-permute-done((bf16[64,4608]{1,0:T(8,128)(2,1)S(1)}, bf16[64,4608]{1,0:T(8,128)(2,1)S(1)}, u32[]{:S(2)}, u32[]{:S(2)}) %collective-permute-start.54) | collective-permute-done | bytes 589856 | tf_op jit(solution)/shard_map/ppermute | solution.py:43
  124.2 4.3 %collective-permute-done.55.refs_2_.refs_6_ = bf16[64,4608]{1,0:T(8,128)(2,1)S(1)} collective-permute-done((bf16[64,4608]{1,0:T(8,128)(2,1)S(1)}, bf16[64,4608]{1,0:T(8,128)(2,1)S(1)}, u32[]{:S(2)}, u32[]{:S(2)}) %collective-permute-start.55) | collective-permute-done | bytes 589856 | tf_op jit(solution)/shard_map/ppermute | solution.py:43
  128.4 2.0 %collective-permute-done.56.refs_3_.refs_7_ = bf16[64,4608]{1,0:T(8,128)(2,1)S(1)} collective-permute-done((bf16[64,4608]{1,0:T(8,128)(2,1)S(1)}, bf16[64,4608]{1,0:T(8,128)(2,1)S(1)}, u32[]{:S(2)}, u32[]{:S(2)}) %collective-permute-start.56) | collective-permute-done | bytes 589856 | tf_op jit(solution)/shard_map/ppermute | solution.py:43
  130.4 2.2 %cross_back.1 = bf16[256,3328]{1,0:T(8,128)(2,1)S(1)} custom-call(s32[6]{0:T(128)S(1)} %stack.27.s, bf16[256,256]{1,0:T(8,128)(2,1)S(1)} %get-tuple-element.160.match_ref, bf16[512,2304]{1,0:T(8,128)(2,1)S(1)} %collective-permute-done.41.cross_first_ref, bf16[512,2304]{1,0:T(8,128)(2,1)S(1)} %copy-done, ...), custom_call_target="tpu_custom_call" | custom-call | flops 2147483648 | bytes 7208960 | tf_op jit(solution)/shard_map/cross_back/pallas_call | solution.py:90
  132.7 4.1 %collective-permute-start.57 = (bf16[256,3328]{1,0:T(8,128)(2,1)S(1)}, bf16[256,3328]{1,0:T(8,128)(2,1)S(1)}, u32[]{:S(2)}, u32[]{:S(2)}) collective-permute-start(bf16[256,3328]{1,0:T(8,128)(2,1)S(1)} %cross_back.1), channel_id=1, source_target_pairs={{64,0},{65,1},{66,2},{67,3},{68,4},{69,5},{70,6},{71,7},{72,8},{73... | collective-permute-start | bytes 5111816 | tf_op jit(solution)/shard_map/ppermute | solution.py:59
  136.8 3.9 %self_back.1 = (f32[256,512]{1,0:T(8,128)S(1)}, bf16[1,512,4608]{2,1,0:T(8,128)(2,1)}) custom-call(s32[6]{0:T(128)S(1)} %stack.27.s, bf16[256,640]{1,0:T(8,128)(2,1)S(1)} %get-tuple-element.134.codes_ref.own_ref, bf16[1,512,4608]{2,1,0:T(8,128)(2,1)S(1)} %bitcast.81, bf16[64,4608]{1,0:T(8,128)(2,1)S(1)} %get-tuple-element.153.refs_0_.refs_4_, ...), custom_call_target="tpu_custom_call" | custom-call | flops 2147483648 | bytes 7405568 | tf_op jit(solution)/shard_map/self_back/pallas_call | solution.py:90
  140.7 4.7 %last.1 = (bf16[1,4608,512]{2,1,0:T(8,128)(2,1)}, f32[1,512]{1,0:T(1,128)}, bf16[512,2304]{1,0:T(8,128)(2,1)}, bf16[64,128]{1,0:T(8,128)(2,1)}, s32[1]{0:T(128)}) custom-call(s32[6]{0:T(128)S(1)} %stack.27.s, f32[256,512]{1,0:T(8,128)S(1)} %get-tuple-element.157.term_ref, f32[256,512]{1,0:T(8,128)S(1)} %get-tuple-element.158.gate_ref, ...), custom_call_target="tpu_custom_call" | custom-call | flops 2147483648 | bytes 7831552 | tf_op jit(solution)/shard_map/last/pallas_call | solution.py:90
  145.5 0.8 while.19
  (49 shorter events, 5.7 us)
Async XLA Ops:
  0.6 2.5 %collective-permute-start.30 = (s32[1,8,8]{2,1,0:T(8,128)}, s32[1,8,8]{2,1,0:T(8,128)S(1)}, u32[]{:S(2)}, u32[]{:S(2)}) collective-permute-start(s32[1,8,8]{2,1,0:T(8,128)} %param.15), channel_id=1, source_target_pairs={{0,64},{64,0},{1,65},{65,1},{2,66},{66,2},{3,67},{67,3},{4,68},{68... | collective-permute-start | bytes 776 | tf_op jit(solution)/shard_map/ppermute | solution.py:63
  4.2 5.0 %collective-permute-start.31 = (bf16[8,4736]{1,0:T(8,128)(2,1)S(1)}, bf16[8,4736]{1,0:T(8,128)(2,1)S(1)}, u32[]{:S(2)}, u32[]{:S(2)}) collective-permute-start(bf16[8,4736]{1,0:T(8,128)(2,1)S(1)} %concatenate.38), channel_id=1, source_target_pairs={{0,32},{1,33},{2,34},{3,35},{4,36},{5,37},{6,38},{7,39},{8,40},{9,... | collective-permute-start | bytes 227336 | tf_op jit(solution)/shard_map/ppermute | solution.py:43
  7.0 3.2 %collective-permute-start.32 = (bf16[8,4736]{1,0:T(8,128)(2,1)S(1)}, bf16[8,4736]{1,0:T(8,128)(2,1)S(1)}, u32[]{:S(2)}, u32[]{:S(2)}) collective-permute-start(bf16[8,4736]{1,0:T(8,128)(2,1)S(1)} %concatenate.38), channel_id=1, source_target_pairs={{0,48},{1,49},{2,50},{3,51},{4,52},{5,53},{6,54},{7,55},{8,56},{9,... | collective-permute-start | bytes 227336 | tf_op jit(solution)/shard_map/ppermute | solution.py:43
  7.9 4.4 %collective-permute-start.33 = (bf16[8,4736]{1,0:T(8,128)(2,1)S(1)}, bf16[8,4736]{1,0:T(8,128)(2,1)S(1)}, u32[]{:S(2)}, u32[]{:S(2)}) collective-permute-start(bf16[8,4736]{1,0:T(8,128)(2,1)S(1)} %concatenate.38), channel_id=1, source_target_pairs={{0,16},{1,17},{2,18},{3,19},{4,20},{5,21},{6,22},{7,23},{8,24},{9,... | collective-permute-start | bytes 227336 | tf_op jit(solution)/shard_map/ppermute | solution.py:43
  12.3 32.6 %copy-start.12 = (f32[1,512]{1,0:T(1,128)S(1)}, f32[1,512]{1,0:T(1,128)}, u32[]{:S(2)}) copy-start(f32[1,512]{1,0:T(1,128)} %refs_5_.1) | copy-start | bytes 6148
  12.3 8.2 %collective-permute-start.34 = (bf16[32,4736]{1,0:T(8,128)(2,1)S(1)}, bf16[32,4736]{1,0:T(8,128)(2,1)S(1)}, u32[]{:S(2)}, u32[]{:S(2)}) collective-permute-start(bf16[32,4736]{1,0:T(8,128)(2,1)S(1)} %pad_maximum_fusion.4.refs_0_), channel_id=1, source_target_pairs={{0,8},{1,9},{2,10},{3,11},{4,12},{5,13},{6,14},{7,15},{8,0},{9,1},... | collective-permute-start | bytes 909320 | tf_op jit(solution)/shard_map/ppermute | solution.py:43
  16.0 8.5 %collective-permute-start.35 = (bf16[32,4736]{1,0:T(8,128)(2,1)S(1)}, bf16[32,4736]{1,0:T(8,128)(2,1)S(1)}, u32[]{:S(2)}, u32[]{:S(2)}) collective-permute-start(bf16[32,4736]{1,0:T(8,128)(2,1)S(1)} %pad_maximum_fusion.4.refs_0_), channel_id=1, source_target_pairs={{0,12},{1,13},{2,14},{3,15},{4,0},{5,1},{6,2},{7,3},{8,4},{9,5},{1... | collective-permute-start | bytes 909320 | tf_op jit(solution)/shard_map/ppermute | solution.py:43
  16.4 8.1 %collective-permute-start.36 = (bf16[32,4736]{1,0:T(8,128)(2,1)S(1)}, bf16[32,4736]{1,0:T(8,128)(2,1)S(1)}, u32[]{:S(2)}, u32[]{:S(2)}) collective-permute-start(bf16[32,4736]{1,0:T(8,128)(2,1)S(1)} %pad_maximum_fusion.4.refs_0_), channel_id=1, source_target_pairs={{0,4},{1,5},{2,6},{3,7},{4,8},{5,9},{6,10},{7,11},{8,12},{9,13},{1... | collective-permute-start | bytes 909320 | tf_op jit(solution)/shard_map/ppermute | solution.py:43
  17.6 26.0 %copy-start = (bf16[512,2304]{1,0:T(8,128)(2,1)S(1)}, bf16[512,2304]{1,0:T(8,128)(2,1)}, u32[]{:S(2)}) copy-start(bf16[512,2304]{1,0:T(8,128)(2,1)} %cross_ref.3) | copy-start | bytes 7077892
  17.6 27.3 %copy-start.11 = (bf16[1,4608,512]{2,1,0:T(8,128)(2,1)S(1)}, bf16[1,4608,512]{2,1,0:T(8,128)(2,1)}, u32[]{:S(2)}) copy-start(bf16[1,4608,512]{2,1,0:T(8,128)(2,1)} %refs_4_.2) | copy-start | bytes 14155780
  24.5 27.2 %slice-start.2 = ((s8[4718592]{0:T(1024)(128)(4,1)}), s8[4194304]{0:T(1024)(128)(4,1)S(1)}, s32[]{:S(2)}) async-start(s8[4718592]{0:T(1024)(128)(4,1)} %bitcast.80), calls=%async_computation.2 | async-start | bytes 8388608
  26.2 10.8 %collective-permute-start.37 = (bf16[64,4736]{1,0:T(8,128)(2,1)S(1)}, bf16[64,4736]{1,0:T(8,128)(2,1)S(1)}, u32[]{:S(2)}, u32[]{:S(2)}) collective-permute-start(bf16[64,4736]{1,0:T(8,128)(2,1)S(1)} %get-tuple-element.126), channel_id=1, source_target_pairs={{0,2},{1,3},{2,0},{3,1},{4,6},{5,7},{6,4},{7,5},{8,10},{9,11},{10,... | collective-permute-start | bytes 1818632 | tf_op jit(solution)/shard_map/ppermute | solution.py:43
  28.9 14.7 %collective-permute-start.38 = (bf16[64,4736]{1,0:T(8,128)(2,1)S(1)}, bf16[64,4736]{1,0:T(8,128)(2,1)S(1)}, u32[]{:S(2)}, u32[]{:S(2)}) collective-permute-start(bf16[64,4736]{1,0:T(8,128)(2,1)S(1)} %get-tuple-element.127), channel_id=1, source_target_pairs={{0,3},{1,0},{2,1},{3,2},{4,7},{5,4},{6,5},{7,6},{8,11},{9,8},{10,9... | collective-permute-start | bytes 1818632 | tf_op jit(solution)/shard_map/ppermute | solution.py:43
  30.0 21.8 %slice-start.3 = ((s8[4718592]{0:T(1024)(128)(4,1)}), s8[524288]{0:T(1024)(128)(4,1)S(1)}, s32[]{:S(2)}) async-start(s8[4718592]{0:T(1024)(128)(4,1)} %bitcast.80), calls=%async_computation.3 | async-start | bytes 1048576
  30.0 13.6 %collective-permute-start.39 = (bf16[64,4736]{1,0:T(8,128)(2,1)S(1)}, bf16[64,4736]{1,0:T(8,128)(2,1)S(1)}, u32[]{:S(2)}, u32[]{:S(2)}) collective-permute-start(bf16[64,4736]{1,0:T(8,128)(2,1)S(1)} %get-tuple-element.128), channel_id=1, source_target_pairs={{0,1},{1,2},{2,3},{3,0},{4,5},{5,6},{6,7},{7,4},{8,9},{9,10},{10,1... | collective-permute-start | bytes 1818632 | tf_op jit(solution)/shard_map/ppermute | solution.py:43
  43.6 10.2 %collective-permute-start.41 = (bf16[512,2304]{1,0:T(8,128)(2,1)S(1)}, bf16[512,2304]{1,0:T(8,128)(2,1)S(1)}, u32[]{:S(2)}, u32[]{:S(2)}) collective-permute-start(bf16[512,2304]{1,0:T(8,128)(2,1)S(1)} %copy-done), channel_id=1, source_target_pairs={{0,64},{1,65},{2,66},{3,67},{4,68},{5,69},{6,70},{7,71},{8,72},{9,... | collective-permute-start | bytes 7077896 | tf_op jit(solution)/shard_map/ppermute | solution.py:55
  47.2 6.6 %collective-permute-start.40 = (bf16[256,640]{1,0:T(8,128)(2,1)S(1)}, bf16[256,640]{1,0:T(8,128)(2,1)S(1)}, u32[]{:S(2)}, u32[]{:S(2)}) collective-permute-start(bf16[256,640]{1,0:T(8,128)(2,1)S(1)} %get-tuple-element.134.codes_ref.own_ref), channel_id=1, source_target_pairs={{0,64},{64,0},{1,65},{65,1},{2,66},{66,2},{3,67},{67,3},{4,68},{68... | collective-permute-start | bytes 983048 | tf_op jit(solution)/shard_map/ppermute | solution.py:63
  53.8 76.7 %copy-start.2 = (bf16[512,2304]{1,0:T(8,128)(2,1)}, bf16[512,2304]{1,0:T(8,128)(2,1)S(1)}, u32[]{:S(2)}) copy-start(bf16[512,2304]{1,0:T(8,128)(2,1)S(1)} %collective-permute-done.41.cross_first_ref) | copy-start | bytes 7077892
  56.2 32.5 %copy-start.8 = (bf16[1,8,4608]{2,1,0:T(8,128)(2,1)S(1)}, bf16[1,8,4608]{2,1,0:T(8,128)(2,1)}, u32[]{:S(2)}) copy-start(bf16[1,8,4608]{2,1,0:T(8,128)(2,1)} %refs_3_.1) | copy-start | bytes 221188
  56.2 11.8 %collective-permute-start.42 = (bf16[64,5632]{1,0:T(8,128)(2,1)S(1)}, bf16[64,5632]{1,0:T(8,128)(2,1)S(1)}, u32[]{:S(2)}, u32[]{:S(2)}) collective-permute-start(bf16[64,5632]{1,0:T(8,128)(2,1)S(1)} %get-tuple-element.141), channel_id=1, source_target_pairs={{0,2},{1,3},{2,0},{3,1},{4,6},{5,7},{6,4},{7,5},{8,10},{9,11},{10,... | collective-permute-start | bytes 2162696 | tf_op jit(solution)/shard_map/ppermute | solution.py:43
  56.5 19.1 %collective-permute-start.43 = (bf16[64,5632]{1,0:T(8,128)(2,1)S(1)}, bf16[64,5632]{1,0:T(8,128)(2,1)S(1)}, u32[]{:S(2)}, u32[]{:S(2)}) collective-permute-start(bf16[64,5632]{1,0:T(8,128)(2,1)S(1)} %get-tuple-element.142), channel_id=1, source_target_pairs={{0,1},{1,2},{2,3},{3,0},{4,5},{5,6},{6,7},{7,4},{8,9},{9,10},{10,1... | collective-permute-start | bytes 2162696 | tf_op jit(solution)/shard_map/ppermute | solution.py:43
  56.6 19.0 %collective-permute-start.44 = (bf16[64,5632]{1,0:T(8,128)(2,1)S(1)}, bf16[64,5632]{1,0:T(8,128)(2,1)S(1)}, u32[]{:S(2)}, u32[]{:S(2)}) collective-permute-start(bf16[64,5632]{1,0:T(8,128)(2,1)S(1)} %get-tuple-element.143), channel_id=1, source_target_pairs={{0,3},{1,0},{2,1},{3,2},{4,7},{5,4},{6,5},{7,6},{8,11},{9,8},{10,9... | collective-permute-start | bytes 2162696 | tf_op jit(solution)/shard_map/ppermute | solution.py:43
  76.7 8.2 %collective-permute-start.45 = (bf16[32,5632]{1,0:T(8,128)(2,1)S(1)}, bf16[32,5632]{1,0:T(8,128)(2,1)S(1)}, u32[]{:S(2)}, u32[]{:S(2)}) collective-permute-start(bf16[32,5632]{1,0:T(8,128)(2,1)S(1)} %get-tuple-element.145), channel_id=1, source_target_pairs={{0,8},{1,9},{2,10},{3,11},{4,12},{5,13},{6,14},{7,15},{8,0},{9,1},... | collective-permute-start | bytes 1081352 | tf_op jit(solution)/shard_map/ppermute | solution.py:43
  79.0 9.8 %collective-permute-start.46 = (bf16[32,5632]{1,0:T(8,128)(2,1)S(1)}, bf16[32,5632]{1,0:T(8,128)(2,1)S(1)}, u32[]{:S(2)}, u32[]{:S(2)}) collective-permute-start(bf16[32,5632]{1,0:T(8,128)(2,1)S(1)} %get-tuple-element.146), channel_id=1, source_target_pairs={{0,4},{1,5},{2,6},{3,7},{4,8},{5,9},{6,10},{7,11},{8,12},{9,13},{1... | collective-permute-start | bytes 1081352 | tf_op jit(solution)/shard_map/ppermute | solution.py:43
  79.7 9.0 %collective-permute-start.47 = (bf16[32,5632]{1,0:T(8,128)(2,1)S(1)}, bf16[32,5632]{1,0:T(8,128)(2,1)S(1)}, u32[]{:S(2)}, u32[]{:S(2)}) collective-permute-start(bf16[32,5632]{1,0:T(8,128)(2,1)S(1)} %get-tuple-element.147), channel_id=1, source_target_pairs={{0,12},{1,13},{2,14},{3,15},{4,0},{5,1},{6,2},{7,3},{8,4},{9,5},{1... | collective-permute-start | bytes 1081352 | tf_op jit(solution)/shard_map/ppermute | solution.py:43
  89.5 7.6 %collective-permute-start.48 = (bf16[32,4864]{1,0:T(8,128)(2,1)S(1)}, bf16[32,4864]{1,0:T(8,128)(2,1)S(1)}, u32[]{:S(2)}, u32[]{:S(2)}) collective-permute-start(bf16[32,4864]{1,0:T(8,128)(2,1)S(1)} %get-tuple-element.149), channel_id=1, source_target_pairs={{0,32},{1,33},{2,34},{3,35},{4,36},{5,37},{6,38},{7,39},{8,40},{9,... | collective-permute-start | bytes 933896 | tf_op jit(solution)/shard_map/ppermute | solution.py:43
  91.6 8.3 %collective-permute-start.49 = (bf16[32,4864]{1,0:T(8,128)(2,1)S(1)}, bf16[32,4864]{1,0:T(8,128)(2,1)S(1)}, u32[]{:S(2)}, u32[]{:S(2)}) collective-permute-start(bf16[32,4864]{1,0:T(8,128)(2,1)S(1)} %get-tuple-element.150), channel_id=1, source_target_pairs={{0,48},{1,49},{2,50},{3,51},{4,52},{5,53},{6,54},{7,55},{8,56},{9,... | collective-permute-start | bytes 933896 | tf_op jit(solution)/shard_map/ppermute | solution.py:43
  92.6 7.9 %collective-permute-start.50 = (bf16[32,4864]{1,0:T(8,128)(2,1)S(1)}, bf16[32,4864]{1,0:T(8,128)(2,1)S(1)}, u32[]{:S(2)}, u32[]{:S(2)}) collective-permute-start(bf16[32,4864]{1,0:T(8,128)(2,1)S(1)} %get-tuple-element.151), channel_id=1, source_target_pairs={{0,16},{1,17},{2,18},{3,19},{4,20},{5,21},{6,22},{7,23},{8,24},{9,... | collective-permute-start | bytes 933896 | tf_op jit(solution)/shard_map/ppermute | solution.py:43
  101.7 7.4 %collective-permute-start.51 = (bf16[32,4608]{1,0:T(8,128)(2,1)S(1)}, bf16[32,4608]{1,0:T(8,128)(2,1)S(1)}, u32[]{:S(2)}, u32[]{:S(2)}) collective-permute-start(bf16[32,4608]{1,0:T(8,128)(2,1)S(1)} %get-tuple-element.152.refs_0_), channel_id=1, source_target_pairs={{0,8},{1,9},{2,10},{3,11},{4,12},{5,13},{6,14},{7,15},{8,0},{9,1},... | collective-permute-start | bytes 884744 | tf_op jit(solution)/shard_map/ppermute | solution.py:43
  103.4 8.8 %collective-permute-start.52 = (bf16[32,4608]{1,0:T(8,128)(2,1)S(1)}, bf16[32,4608]{1,0:T(8,128)(2,1)S(1)}, u32[]{:S(2)}, u32[]{:S(2)}) collective-permute-start(bf16[32,4608]{1,0:T(8,128)(2,1)S(1)} %get-tuple-element.152.refs_0_), channel_id=1, source_target_pairs={{0,12},{1,13},{2,14},{3,15},{4,0},{5,1},{6,2},{7,3},{8,4},{9,5},{1... | collective-permute-start | bytes 884744 | tf_op jit(solution)/shard_map/ppermute | solution.py:43
  104.8 7.4 %collective-permute-start.53 = (bf16[32,4608]{1,0:T(8,128)(2,1)S(1)}, bf16[32,4608]{1,0:T(8,128)(2,1)S(1)}, u32[]{:S(2)}, u32[]{:S(2)}) collective-permute-start(bf16[32,4608]{1,0:T(8,128)(2,1)S(1)} %get-tuple-element.152.refs_0_), channel_id=1, source_target_pairs={{0,4},{1,5},{2,6},{3,7},{4,8},{5,9},{6,10},{7,11},{8,12},{9,13},{1... | collective-permute-start | bytes 884744 | tf_op jit(solution)/shard_map/ppermute | solution.py:43
  113.5 10.7 %collective-permute-start.54 = (bf16[64,4608]{1,0:T(8,128)(2,1)S(1)}, bf16[64,4608]{1,0:T(8,128)(2,1)S(1)}, u32[]{:S(2)}, u32[]{:S(2)}) collective-permute-start(bf16[64,4608]{1,0:T(8,128)(2,1)S(1)} %get-tuple-element.154), channel_id=1, source_target_pairs={{0,2},{1,3},{2,0},{3,1},{4,6},{5,7},{6,4},{7,5},{8,10},{9,11},{10,... | collective-permute-start | bytes 1769480 | tf_op jit(solution)/shard_map/ppermute | solution.py:43
  113.6 14.9 %collective-permute-start.55 = (bf16[64,4608]{1,0:T(8,128)(2,1)S(1)}, bf16[64,4608]{1,0:T(8,128)(2,1)S(1)}, u32[]{:S(2)}, u32[]{:S(2)}) collective-permute-start(bf16[64,4608]{1,0:T(8,128)(2,1)S(1)} %get-tuple-element.155), channel_id=1, source_target_pairs={{0,3},{1,0},{2,1},{3,2},{4,7},{5,4},{6,5},{7,6},{8,11},{9,8},{10,9... | collective-permute-start | bytes 1769480 | tf_op jit(solution)/shard_map/ppermute | solution.py:43
  115.3 15.2 %collective-permute-start.56 = (bf16[64,4608]{1,0:T(8,128)(2,1)S(1)}, bf16[64,4608]{1,0:T(8,128)(2,1)S(1)}, u32[]{:S(2)}, u32[]{:S(2)}) collective-permute-start(bf16[64,4608]{1,0:T(8,128)(2,1)S(1)} %get-tuple-element.156), channel_id=1, source_target_pairs={{0,1},{1,2},{2,3},{3,0},{4,5},{5,6},{6,7},{7,4},{8,9},{9,10},{10,1... | collective-permute-start | bytes 1769480 | tf_op jit(solution)/shard_map/ppermute | solution.py:43
  132.7 8.1 %collective-permute-start.57 = (bf16[256,3328]{1,0:T(8,128)(2,1)S(1)}, bf16[256,3328]{1,0:T(8,128)(2,1)S(1)}, u32[]{:S(2)}, u32[]{:S(2)}) collective-permute-start(bf16[256,3328]{1,0:T(8,128)(2,1)S(1)} %cross_back.1), channel_id=1, source_target_pairs={{64,0},{65,1},{66,2},{67,3},{68,4},{69,5},{70,6},{71,7},{72,8},{73... | collective-permute-start | bytes 5111816 | tf_op jit(solution)/shard_map/ppermute | solution.py:59
  140.7 4.8 %copy-start.7 = (bf16[1,8,4608]{2,1,0:T(8,128)(2,1)S(1)}, bf16[1,8,4608]{2,1,0:T(8,128)(2,1)}, u32[]{:S(2)}) copy-start(bf16[1,8,4608]{2,1,0:T(8,128)(2,1)} %param.9) | copy-start | bytes 221188
  140.7 4.8 %copy-start.9 = (bf16[1,8,4608]{2,1,0:T(8,128)(2,1)S(1)}, bf16[1,8,4608]{2,1,0:T(8,128)(2,1)}, u32[]{:S(2)}) copy-start(bf16[1,8,4608]{2,1,0:T(8,128)(2,1)} %refs_3_.1) | copy-start | bytes 221188
  140.7 4.8 %copy-start.10 = (s32[1,8,8]{2,1,0:T(8,128)S(1)}, s32[1,8,8]{2,1,0:T(8,128)}, u32[]{:S(2)}) copy-start(s32[1,8,8]{2,1,0:T(8,128)} %param.15) | copy-start | bytes 772
where the time goes:
time: 147 us
  waiting for transfers between devices  77.7 us (53%)
  starting transfers between devices  41.6 us (28%)
  Pallas kernels  23.6 us (16%)
    ppermute x24, waiting for transfers between devices, send(): return lax.ppermute(block, ('layer', 'feat'), route(axes, distance))  77.3 us
    ppermute x24, starting transfers between devices, send(): return lax.ppermute(block, ('layer', 'feat'), route(axes, distance))  30.1 us
    pallas_call x11, Pallas kernels, call(): pl.pallas_call(kernel, in_specs=[smem] + [vmem] * len(ins), out_specs=[pl...  23.6 us
    ppermute x2, starting transfers between devices, swapped(): return lax.ppermute(block, 'layer', [(0, 1), (1, 0)])  6.1 us
    ppermute x1, starting transfers between devices, to_first(): return lax.ppermute(block, 'layer', [(1, 0)])  4.09 us
  transfers between devices with their start and end apart: 28, of which 20 were waited for; matrix products, arithmetic and copies ran while one was open for 1% of the time, Pallas kernels for 6%

commit v1 on v0

--- a/solution.py
+++ b/solution.py
@@ -337,8 +337,8 @@
 
 
 def settle_kernel(s, exact_ref, *refs):
-    came, targets_ref, err_ref, recon_ref, tail_ref = refs[:3], *refs[3:]
-    tokens, width = targets_ref.shape[1:]
+    came, err_ref, own_ref, tail_ref = refs[:3], *refs[3:]
+    tokens, width = own_ref.shape
     for cols in sixths(width):
         total = exact_ref[:, cols]
         for r in (1, 2, 3):
@@ -346,7 +346,7 @@
             order = [AWAY.index((AWAY[j] - AWAY[r]) % SIDE) for j in range(SIDE)]
             total += jnp.concatenate([value[tokens * i : tokens * (i + 1)] for i in order], axis=0)
         err_ref[:, cols] = total.astype(BF16)
-        recon_ref[0, :, cols] = total[:tokens] + targets_ref[0, :, cols].astype(F32)
+        own_ref[:, cols] = total[:tokens]
     slots = tail_ref.shape[1]
     tail = exact_ref[0:tokens, pl.ds(width, slots)]
     for r in (1, 2, 3):
@@ -355,11 +355,10 @@
     tail_ref[...] = tail
 
 
-def settle(scalars, exact, came, targets):
+def settle(scalars, exact, came, tokens, width):
     rows, columns = exact.shape
-    tokens, width = targets.shape[1:]
-    outs = [((rows, width), BF16), ((1, tokens, width), F32), ((tokens, columns - width), F32)]
-    return call(settle_kernel, "settle", scalars, [exact, *came, targets], outs)
+    outs = [((rows, width), BF16), ((tokens, width), F32), ((tokens, columns - width), F32)]
+    return call(settle_kernel, "settle", scalars, [exact, *came], outs)
 
 
 def compact_kernel(s, pick_ref, *refs):
@@ -426,10 +425,10 @@
     return call(self_kernel, "self_back", scalars, [codes, w_self, *pieces], outs, scratch)
 
 
-def last_kernel(s, term_ref, gate_ref, source_ref, returned_ref, tail_ref, *refs):
+def last_kernel(s, term_ref, gate_ref, source_ref, returned_ref, tail_ref, own_ref, targets_ref, *refs):
     x, errs = refs[:4], refs[4:8]
-    enc_ref, bias_ref, cross_ref, picked_ref, again_ref = refs[8:13]
-    dpre, turned, enc, cross, sems = refs[13:]
+    enc_ref, bias_ref, cross_ref, picked_ref, recon_ref, again_ref = refs[8:14]
+    dpre, turned, enc, cross, bias, picked, recon, sems = refs[14:]
     width, half = enc.shape[0], cross.shape[1]
     writer = Writer(sems)
     latents = dpre.shape[1]
@@ -437,13 +436,17 @@
     back = [returned_ref[:, pl.ds(at, latents)].astype(F32) for at in (half, half + latents)]
     value = ((term_ref[...] + (back[0] + back[1])) * gate_ref[...]).astype(BF16)
     dpre[...] = value
-    bias_ref[...] = jnp.sum(value.astype(F32), axis=0, keepdims=True)
+    bias[...] = jnp.sum(value.astype(F32), axis=0, keepdims=True)
+    writer.write(bias, bias_ref)
+    recon[...] = own_ref[...] + targets_ref[0].astype(F32)
+    writer.write(recon, recon_ref.at[0])
+    tokens, slots = tail_ref.shape[0], tail_ref.shape[1] // BLK
+    rows = [tail_ref[t : t + 1, pl.ds(k * BLK, BLK)] for t in range(tokens) for k in range(slots)]
+    picked[...] = jnp.concatenate(rows, axis=0).astype(BF16)
+    writer.write(picked, picked_ref)
     for cols in sixths(width):
         enc[cols, :] = contract_rows(stacked(x, cols), dpre[...]).astype(BF16)
         writer.write(enc.at[cols, :], enc_ref.at[0, cols, :])
-    tokens, slots = tail_ref.shape[0], tail_ref.shape[1] // BLK
-    rows = [tail_ref[t : t + 1, pl.ds(k * BLK, BLK)] for t in range(tokens) for k in range(slots)]
-    picked_ref[...] = jnp.concatenate(rows, axis=0).astype(BF16)
     turned[...] = source_ref[...].T
     step = half // 3
     for j in range(3):
@@ -462,15 +465,16 @@
     writer.finish()
 
 
-def last(scalars, term, gate, source, returned, tail, x, errs):
+def last(scalars, term, gate, source, returned, tail, own_err, targets, x, errs):
     latents, half = source.shape[1], returned.shape[1] - 2 * source.shape[1]
-    picked = tail.shape[0] * tail.shape[1] // BLK
-    outs = [((1, 2 * half, latents), BF16, pltpu.HBM), ((1, latents), F32), ((latents, half), BF16, pltpu.HBM)]
-    outs += [((picked, BLK), BF16), ((1,), jnp.int32, pltpu.SMEM)]
-    scratch = [pltpu.VMEM((ROWS, latents), BF16), pltpu.VMEM((latents, ROWS), BF16)]
-    scratch += [pltpu.VMEM((2 * half, latents), BF16), pltpu.VMEM((latents, half), BF16)]
-    scratch += [pltpu.SemaphoreType.DMA((9,))]
-    ins = [term, gate, source, returned, tail, *x, *errs]
+    picked = ((tail.shape[0] * tail.shape[1] // BLK, BLK), BF16)
+    enc, bias, cross = ((2 * half, latents), BF16), ((1, latents), F32), ((latents, half), BF16)
+    recon = (own_err.shape, F32)
+    outs = [((1, *enc[0]), BF16), bias, cross, picked, ((1, *recon[0]), F32)]
+    outs = [(*out, pltpu.HBM) for out in outs] + [((1,), jnp.int32, pltpu.SMEM)]
+    scratch = [((ROWS, latents), BF16), ((latents, ROWS), BF16), enc, cross, bias, picked, recon]
+    scratch = [pltpu.VMEM(*what) for what in scratch] + [pltpu.SemaphoreType.DMA((12,))]
+    ins = [term, gate, source, returned, tail, own_err, targets, *x, *errs]
     return call(last_kernel, "last", scalars, ins, outs, scratch)
 
 
@@ -568,13 +572,15 @@
     sums, source, match = decode(scalars, codes, other_codes, self_sum, w_cross_first, w_cross, slotted)
     sums = behind(sums, OUTER)
     exact, sents = line_terms(scalars, behind(spread_sum(scalars, spread, sums, width), MIDDLE), targets)
-    err_line, recon, tail = settle(scalars, exact, ahead(exact, sents, INNER)[1:], targets)
+    err_line, own_err, tail = settle(scalars, exact, ahead(exact, sents, INNER)[1:], tokens_dev, width)
     err_plane = line_gather(err_line, MIDDLE)
     kept = compact(scalars, pick, err_plane)
     errs = ahead(kept[0], kept, OUTER)
     returned = to_first(cross_back(scalars, match, errs, w_cross_first, w_cross))
     term, grad_self = self_back(scalars, codes, errs, w_self)
-    grad_enc, grad_benc, grad_cross, picked, again = last(scalars, term, gate, source, returned, tail, x, errs)
+    grad_enc, grad_benc, grad_cross, picked, recon, again = last(
+        scalars, term, gate, source, returned, tail, own_err, targets, x, errs
+    )
 
     def on_every_row(_):
         results = dense(inputs, targets, w_enc, b_enc, w_self, w_cross, block_ids, w_cross_first)

time: 147 us -> 146 us (level)
  no operation moved by 1% of the time
where the time goes in v1:
time: 146 us
  waiting for transfers between devices  77.6 us (53%)
  starting transfers between devices  41.7 us (29%)
  Pallas kernels  22.9 us (16%)
    ppermute x24, waiting for transfers between devices, send(): return lax.ppermute(block, ('layer', 'feat'), route(axes, distance))  77.3 us
    ppermute x24, starting transfers between devices, send(): return lax.ppermute(block, ('layer', 'feat'), route(axes, distance))  30.2 us
    pallas_call x11, Pallas kernels, call(): pl.pallas_call(kernel, in_specs=[smem] + [vmem] * len(ins), out_specs=[pl...  22.9 us
    ppermute x2, starting transfers between devices, swapped(): return lax.ppermute(block, 'layer', [(0, 1), (1, 0)])  6.1 us
    ppermute x1, starting transfers between devices, to_first(): return lax.ppermute(block, 'layer', [(1, 0)])  4.09 us
  transfers between devices with their start and end apart: 28, of which 20 were waited for; matrix products, arithmetic and copies ran while one was open for 1% of the time, Pallas kernels for 6%

profile of v1, /device:TPU:1, one launch (start us, length us, event | category | flops | bytes accessed | tf_op | source)
XLA Modules:
  0.0 146.0 jit_solution(2188001721981091130)
XLA Ops:
  0.6 1.5 %collective-permute-start.30 = (s32[1,8,8]{2,1,0:T(8,128)}, s32[1,8,8]{2,1,0:T(8,128)S(1)}, u32[]{:S(2)}, u32[]{:S(2)}) collective-permute-start(s32[1,8,8]{2,1,0:T(8,128)} %param.15), channel_id=1, source_target_pairs={{0,64},{64,0},{1,65},{65,1},{2,66},{66,2},{3,67},{67,3},{4,68},{68... | collective-permute-start | bytes 776 | tf_op jit(solution)/shard_map/ppermute | solution.py:63
  3.2 1.0 concatenate.38
  4.2 2.8 %collective-permute-start.31 = (bf16[8,4736]{1,0:T(8,128)(2,1)S(1)}, bf16[8,4736]{1,0:T(8,128)(2,1)S(1)}, u32[]{:S(2)}, u32[]{:S(2)}) collective-permute-start(bf16[8,4736]{1,0:T(8,128)(2,1)S(1)} %concatenate.38), channel_id=1, source_target_pairs={{0,32},{1,33},{2,34},{3,35},{4,36},{5,37},{6,38},{7,39},{8,40},{9,... | collective-permute-start | bytes 227336 | tf_op jit(solution)/shard_map/ppermute | solution.py:43
  7.0 0.9 collective-permute-start.32
  8.5 0.7 collective-permute-done.31
  9.2 1.0 collective-permute-done.32
  10.2 2.1 %collective-permute-done.33 = bf16[8,4736]{1,0:T(8,128)(2,1)S(1)} collective-permute-done((bf16[8,4736]{1,0:T(8,128)(2,1)S(1)}, bf16[8,4736]{1,0:T(8,128)(2,1)S(1)}, u32[]{:S(2)}, u32[]{:S(2)}) %collective-permute-start.33) | collective-permute-done | bytes 75808 | tf_op jit(solution)/shard_map/ppermute | solution.py:43
  12.3 3.7 %collective-permute-start.34 = (bf16[32,4736]{1,0:T(8,128)(2,1)S(1)}, bf16[32,4736]{1,0:T(8,128)(2,1)S(1)}, u32[]{:S(2)}, u32[]{:S(2)}) collective-permute-start(bf16[32,4736]{1,0:T(8,128)(2,1)S(1)} %pad_maximum_fusion.4.refs_0_), channel_id=1, source_target_pairs={{0,8},{1,9},{2,10},{3,11},{4,12},{5,13},{6,14},{7,15},{8,0},{9,1},... | collective-permute-start | bytes 909320 | tf_op jit(solution)/shard_map/ppermute | solution.py:43
  16.4 1.0 collective-permute-start.36
  17.6 2.9 %collective-permute-done.34.refs_1_ = bf16[32,4736]{1,0:T(8,128)(2,1)S(1)} collective-permute-done((bf16[32,4736]{1,0:T(8,128)(2,1)S(1)}, bf16[32,4736]{1,0:T(8,128)(2,1)S(1)}, u32[]{:S(2)}, u32[]{:S(2)}) %collective-permute-start.34) | collective-permute-done | bytes 303136 | tf_op jit(solution)/shard_map/ppermute | solution.py:43
  20.5 4.0 %collective-permute-done.35.refs_2_ = bf16[32,4736]{1,0:T(8,128)(2,1)S(1)} collective-permute-done((bf16[32,4736]{1,0:T(8,128)(2,1)S(1)}, bf16[32,4736]{1,0:T(8,128)(2,1)S(1)}, u32[]{:S(2)}, u32[]{:S(2)}) %collective-permute-start.35) | collective-permute-done | bytes 303136 | tf_op jit(solution)/shard_map/ppermute | solution.py:43
  24.5 1.7 %select.26 = (bf16[64,4736]{1,0:T(8,128)(2,1)S(1)}, bf16[64,4736]{1,0:T(8,128)(2,1)S(1)}, bf16[64,4736]{1,0:T(8,128)(2,1)S(1)}, bf16[64,4736]{1,0:T(8,128)(2,1)S...) custom-call(s32[6]{0:T(128)S(1)} %stack.27.s, ...), custom_call_target="tpu_custom_call" | custom-call | flops 2147483648 | bytes 1212416 | tf_op jit(solution)/shard_map/select/pallas_call | solution.py:90
  26.2 2.7 %collective-permute-start.37 = (bf16[64,4736]{1,0:T(8,128)(2,1)S(1)}, bf16[64,4736]{1,0:T(8,128)(2,1)S(1)}, u32[]{:S(2)}, u32[]{:S(2)}) collective-permute-start(bf16[64,4736]{1,0:T(8,128)(2,1)S(1)} %get-tuple-element.127), channel_id=1, source_target_pairs={{0,2},{1,3},{2,0},{3,1},{4,6},{5,7},{6,4},{7,5},{8,10},{9,11},{10,... | collective-permute-start | bytes 1818632 | tf_op jit(solution)/shard_map/ppermute | solution.py:43
  28.9 1.1 collective-permute-start.38
  30.4 6.7 %collective-permute-done.37.refs_1_ = bf16[64,4736]{1,0:T(8,128)(2,1)S(1)} collective-permute-done((bf16[64,4736]{1,0:T(8,128)(2,1)S(1)}, bf16[64,4736]{1,0:T(8,128)(2,1)S(1)}, u32[]{:S(2)}, u32[]{:S(2)}) %collective-permute-start.37) | collective-permute-done | bytes 606240 | tf_op jit(solution)/shard_map/ppermute | solution.py:43
  37.1 6.5 %collective-permute-done.38.refs_2_ = bf16[64,4736]{1,0:T(8,128)(2,1)S(1)} collective-permute-done((bf16[64,4736]{1,0:T(8,128)(2,1)S(1)}, bf16[64,4736]{1,0:T(8,128)(2,1)S(1)}, u32[]{:S(2)}, u32[]{:S(2)}) %collective-permute-start.38) | collective-permute-done | bytes 606240 | tf_op jit(solution)/shard_map/ppermute | solution.py:43
  43.6 1.3 collective-permute-start.41
  44.9 2.3 %encode.1 = (bf16[256,640]{1,0:T(8,128)(2,1)S(1)}, f32[256,512]{1,0:T(8,128)S(1)}) custom-call(s32[6]{0:T(128)S(1)} %stack.27.s, bf16[64,4736]{1,0:T(8,128)(2,1)S(1)} %get-tuple-element.130.refs_0_, bf16[64,4736]{1,0:T(8,128)(2,1)S(1)} %collective-permute-done.37.refs_1_, bf16[64,4736]{1,0:T(8,128)(2,1)S(1)} %collective-permute-done.38.refs_2_, ...), custom_call_target="tpu_custom_call" | custom-call | flops 2147483648 | bytes 7161856 | tf_op jit(solution)/shard_map/encode/pallas_call | solution.py:90
  47.2 4.6 %collective-permute-start.40 = (bf16[256,640]{1,0:T(8,128)(2,1)S(1)}, bf16[256,640]{1,0:T(8,128)(2,1)S(1)}, u32[]{:S(2)}, u32[]{:S(2)}) collective-permute-start(bf16[256,640]{1,0:T(8,128)(2,1)S(1)} %get-tuple-element.135.codes_ref.own_ref), channel_id=1, source_target_pairs={{0,64},{64,0},{1,65},{65,1},{2,66},{66,2},{3,67},{67,3},{4,68},{68... | collective-permute-start | bytes 983048 | tf_op jit(solution)/shard_map/ppermute | solution.py:63
  51.8 2.0 %decode_self.1 = (f32[256,4608]{1,0:T(8,128)S(1)}, bf16[256,1024]{1,0:T(8,128)(2,1)S(1)}) custom-call(s32[6]{0:T(128)S(1)} %stack.27.s, bf16[256,640]{1,0:T(8,128)(2,1)S(1)} %get-tuple-element.135.codes_ref.own_ref, bf16[1,512,4608]{2,1,0:T(8,128)(2,1)S(1)} %bitcast.81), custom_call_target="tpu_custom_call" | custom-call | flops 2147483648 | bytes 5046272 | tf_op jit(solution)/shard_map/decode_self/pallas_call | solution.py:90
  53.8 2.4 %decode.1 = (bf16[64,5632]{1,0:T(8,128)(2,1)S(1)}, bf16[64,5632]{1,0:T(8,128)(2,1)S(1)}, bf16[64,5632]{1,0:T(8,128)(2,1)S(1)}, bf16[64,5632]{1,0:T(8,128)(2,1)S(...) custom-call(s32[6]{0:T(128)S(1)} %stack.27.s, bf16[256,640]{1,0:T(8,128)(2,1)S(1)} %get-tuple-element.135.codes_ref.own_ref, ...), custom_call_target="tpu_custom_call" | custom-call | flops 2147483648 | bytes 10616832 | tf_op jit(solution)/shard_map/decode/pallas_call | solution.py:90
  56.6 2.6 %collective-permute-start.44 = (bf16[64,5632]{1,0:T(8,128)(2,1)S(1)}, bf16[64,5632]{1,0:T(8,128)(2,1)S(1)}, u32[]{:S(2)}, u32[]{:S(2)}) collective-permute-start(bf16[64,5632]{1,0:T(8,128)(2,1)S(1)} %get-tuple-element.144), channel_id=1, source_target_pairs={{0,3},{1,0},{2,1},{3,2},{4,7},{5,4},{6,5},{7,6},{8,11},{9,8},{10,9... | collective-permute-start | bytes 2162696 | tf_op jit(solution)/shard_map/ppermute | solution.py:43
  59.2 8.9 %collective-permute-done.42.refs_1_ = bf16[64,5632]{1,0:T(8,128)(2,1)S(1)} collective-permute-done((bf16[64,5632]{1,0:T(8,128)(2,1)S(1)}, bf16[64,5632]{1,0:T(8,128)(2,1)S(1)}, u32[]{:S(2)}, u32[]{:S(2)}) %collective-permute-start.42) | collective-permute-done | bytes 720928 | tf_op jit(solution)/shard_map/ppermute | solution.py:43
  68.0 7.5 %collective-permute-done.43.refs_2_ = bf16[64,5632]{1,0:T(8,128)(2,1)S(1)} collective-permute-done((bf16[64,5632]{1,0:T(8,128)(2,1)S(1)}, bf16[64,5632]{1,0:T(8,128)(2,1)S(1)}, u32[]{:S(2)}, u32[]{:S(2)}) %collective-permute-start.43) | collective-permute-done | bytes 720928 | tf_op jit(solution)/shard_map/ppermute | solution.py:43
  75.6 1.1 spread.1
  76.7 2.3 %collective-permute-start.45 = (bf16[32,5632]{1,0:T(8,128)(2,1)S(1)}, bf16[32,5632]{1,0:T(8,128)(2,1)S(1)}, u32[]{:S(2)}, u32[]{:S(2)}) collective-permute-start(bf16[32,5632]{1,0:T(8,128)(2,1)S(1)} %get-tuple-element.146), channel_id=1, source_target_pairs={{0,8},{1,9},{2,10},{3,11},{4,12},{5,13},{6,14},{7,15},{8,0},{9,1},... | collective-permute-start | bytes 1081352 | tf_op jit(solution)/shard_map/ppermute | solution.py:43
  79.0 0.7 collective-permute-start.46
  79.7 1.9 %collective-permute-start.47 = (bf16[32,5632]{1,0:T(8,128)(2,1)S(1)}, bf16[32,5632]{1,0:T(8,128)(2,1)S(1)}, u32[]{:S(2)}, u32[]{:S(2)}) collective-permute-start(bf16[32,5632]{1,0:T(8,128)(2,1)S(1)} %get-tuple-element.148), channel_id=1, source_target_pairs={{0,12},{1,13},{2,14},{3,15},{4,0},{5,1},{6,2},{7,3},{8,4},{9,5},{1... | collective-permute-start | bytes 1081352 | tf_op jit(solution)/shard_map/ppermute | solution.py:43
  81.6 3.3 %collective-permute-done.45.refs_1_ = bf16[32,5632]{1,0:T(8,128)(2,1)S(1)} collective-permute-done((bf16[32,5632]{1,0:T(8,128)(2,1)S(1)}, bf16[32,5632]{1,0:T(8,128)(2,1)S(1)}, u32[]{:S(2)}, u32[]{:S(2)}) %collective-permute-start.45) | collective-permute-done | bytes 360480 | tf_op jit(solution)/shard_map/ppermute | solution.py:43
  84.9 3.8 %collective-permute-done.46.refs_2_ = bf16[32,5632]{1,0:T(8,128)(2,1)S(1)} collective-permute-done((bf16[32,5632]{1,0:T(8,128)(2,1)S(1)}, bf16[32,5632]{1,0:T(8,128)(2,1)S(1)}, u32[]{:S(2)}, u32[]{:S(2)}) %collective-permute-start.46) | collective-permute-done | bytes 360480 | tf_op jit(solution)/shard_map/ppermute | solution.py:43
  89.5 2.2 %collective-permute-start.48 = (bf16[32,4864]{1,0:T(8,128)(2,1)S(1)}, bf16[32,4864]{1,0:T(8,128)(2,1)S(1)}, u32[]{:S(2)}, u32[]{:S(2)}) collective-permute-start(bf16[32,4864]{1,0:T(8,128)(2,1)S(1)} %get-tuple-element.150), channel_id=1, source_target_pairs={{0,32},{1,33},{2,34},{3,35},{4,36},{5,37},{6,38},{7,39},{8,40},{9,... | collective-permute-start | bytes 933896 | tf_op jit(solution)/shard_map/ppermute | solution.py:43
  91.6 0.9 collective-permute-start.49
  93.1 4.0 %collective-permute-done.48.refs_0_ = bf16[32,4864]{1,0:T(8,128)(2,1)S(1)} collective-permute-done((bf16[32,4864]{1,0:T(8,128)(2,1)S(1)}, bf16[32,4864]{1,0:T(8,128)(2,1)S(1)}, u32[]{:S(2)}, u32[]{:S(2)}) %collective-permute-start.48) | collective-permute-done | bytes 311328 | tf_op jit(solution)/shard_map/ppermute | solution.py:43
  97.1 2.8 %collective-permute-done.49.refs_1_ = bf16[32,4864]{1,0:T(8,128)(2,1)S(1)} collective-permute-done((bf16[32,4864]{1,0:T(8,128)(2,1)S(1)}, bf16[32,4864]{1,0:T(8,128)(2,1)S(1)}, u32[]{:S(2)}, u32[]{:S(2)}) %collective-permute-start.49) | collective-permute-done | bytes 311328 | tf_op jit(solution)/shard_map/ppermute | solution.py:43
  101.1 1.8 %collective-permute-start.51 = (bf16[32,4608]{1,0:T(8,128)(2,1)S(1)}, bf16[32,4608]{1,0:T(8,128)(2,1)S(1)}, u32[]{:S(2)}, u32[]{:S(2)}) collective-permute-start(bf16[32,4608]{1,0:T(8,128)(2,1)S(1)} %get-tuple-element.153.refs_0_), channel_id=1, source_target_pairs={{0,8},{1,9},{2,10},{3,11},{4,12},{5,13},{6,14},{7,15},{8,0},{9,1},... | collective-permute-start | bytes 884744 | tf_op jit(solution)/shard_map/ppermute | solution.py:43
  102.9 1.4 collective-permute-start.52
  104.4 4.2 %collective-permute-done.51.refs_1_ = bf16[32,4608]{1,0:T(8,128)(2,1)S(1)} collective-permute-done((bf16[32,4608]{1,0:T(8,128)(2,1)S(1)}, bf16[32,4608]{1,0:T(8,128)(2,1)S(1)}, u32[]{:S(2)}, u32[]{:S(2)}) %collective-permute-start.51) | collective-permute-done | bytes 294944 | tf_op jit(solution)/shard_map/ppermute | solution.py:43
  108.6 3.2 %collective-permute-done.52.refs_2_ = bf16[32,4608]{1,0:T(8,128)(2,1)S(1)} collective-permute-done((bf16[32,4608]{1,0:T(8,128)(2,1)S(1)}, bf16[32,4608]{1,0:T(8,128)(2,1)S(1)}, u32[]{:S(2)}, u32[]{:S(2)}) %collective-permute-start.52) | collective-permute-done | bytes 294944 | tf_op jit(solution)/shard_map/ppermute | solution.py:43
  111.7 1.3 compact.1
  113.1 1.7 %collective-permute-start.55 = (bf16[64,4608]{1,0:T(8,128)(2,1)S(1)}, bf16[64,4608]{1,0:T(8,128)(2,1)S(1)}, u32[]{:S(2)}, u32[]{:S(2)}) collective-permute-start(bf16[64,4608]{1,0:T(8,128)(2,1)S(1)} %get-tuple-element.156), channel_id=1, source_target_pairs={{0,3},{1,0},{2,1},{3,2},{4,7},{5,4},{6,5},{7,6},{8,11},{9,8},{10,9... | collective-permute-start | bytes 1769480 | tf_op jit(solution)/shard_map/ppermute | solution.py:43
  114.8 8.9 %collective-permute-done.54.refs_1_.refs_5_ = bf16[64,4608]{1,0:T(8,128)(2,1)S(1)} collective-permute-done((bf16[64,4608]{1,0:T(8,128)(2,1)S(1)}, bf16[64,4608]{1,0:T(8,128)(2,1)S(1)}, u32[]{:S(2)}, u32[]{:S(2)}) %collective-permute-start.54) | collective-permute-done | bytes 589856 | tf_op jit(solution)/shard_map/ppermute | solution.py:43
  123.7 4.3 %collective-permute-done.55.refs_2_.refs_6_ = bf16[64,4608]{1,0:T(8,128)(2,1)S(1)} collective-permute-done((bf16[64,4608]{1,0:T(8,128)(2,1)S(1)}, bf16[64,4608]{1,0:T(8,128)(2,1)S(1)}, u32[]{:S(2)}, u32[]{:S(2)}) %collective-permute-start.55) | collective-permute-done | bytes 589856 | tf_op jit(solution)/shard_map/ppermute | solution.py:43
  128.0 2.0 %collective-permute-done.56.refs_3_.refs_7_ = bf16[64,4608]{1,0:T(8,128)(2,1)S(1)} collective-permute-done((bf16[64,4608]{1,0:T(8,128)(2,1)S(1)}, bf16[64,4608]{1,0:T(8,128)(2,1)S(1)}, u32[]{:S(2)}, u32[]{:S(2)}) %collective-permute-start.56) | collective-permute-done | bytes 589856 | tf_op jit(solution)/shard_map/ppermute | solution.py:43
  129.9 2.2 %cross_back.1 = bf16[256,3328]{1,0:T(8,128)(2,1)S(1)} custom-call(s32[6]{0:T(128)S(1)} %stack.27.s, bf16[256,256]{1,0:T(8,128)(2,1)S(1)} %get-tuple-element.161.match_ref, bf16[512,2304]{1,0:T(8,128)(2,1)S(1)} %collective-permute-done.41.cross_first_ref, bf16[512,2304]{1,0:T(8,128)(2,1)S(1)} %copy-done, ...), custom_call_target="tpu_custom_call" | custom-call | flops 2147483648 | bytes 7208960 | tf_op jit(solution)/shard_map/cross_back/pallas_call | solution.py:90
  132.2 4.1 %collective-permute-start.57 = (bf16[256,3328]{1,0:T(8,128)(2,1)S(1)}, bf16[256,3328]{1,0:T(8,128)(2,1)S(1)}, u32[]{:S(2)}, u32[]{:S(2)}) collective-permute-start(bf16[256,3328]{1,0:T(8,128)(2,1)S(1)} %cross_back.1), channel_id=1, source_target_pairs={{64,0},{65,1},{66,2},{67,3},{68,4},{69,5},{70,6},{71,7},{72,8},{73... | collective-permute-start | bytes 5111816 | tf_op jit(solution)/shard_map/ppermute | solution.py:59
  136.3 3.9 %self_back.1 = (f32[256,512]{1,0:T(8,128)S(1)}, bf16[1,512,4608]{2,1,0:T(8,128)(2,1)}) custom-call(s32[6]{0:T(128)S(1)} %stack.27.s, bf16[256,640]{1,0:T(8,128)(2,1)S(1)} %get-tuple-element.135.codes_ref.own_ref, bf16[1,512,4608]{2,1,0:T(8,128)(2,1)S(1)} %bitcast.81, bf16[64,4608]{1,0:T(8,128)(2,1)S(1)} %get-tuple-element.154.refs_0_.refs_4_, ...), custom_call_target="tpu_custom_call" | custom-call | flops 2147483648 | bytes 7405568 | tf_op jit(solution)/shard_map/self_back/pallas_call | solution.py:90
  140.2 4.7 %last.1 = (bf16[1,4608,512]{2,1,0:T(8,128)(2,1)}, f32[1,512]{1,0:T(1,128)}, bf16[512,2304]{1,0:T(8,128)(2,1)}, bf16[64,128]{1,0:T(8,128)(2,1)}, f32[1,8,4608]{2,1,0:T(8,128)}, /*index=5*/s32[1]{0:T(128)}) custom-call(s32[6]{0:T(128)S(1)} %stack.27.s, f32[256,512]{1,0:T(8,128)S(1)} %get-tuple-element.158.term_ref, ...), custom_call_target="tpu_custom_call" | custom-call | flops 2147483648 | bytes 8052736 | tf_op jit(solution)/shard_map/last/pallas_call | solution.py:90
  144.9 0.9 while.19
  (47 shorter events, 5.6 us)
Async XLA Ops:
  0.6 2.5 %collective-permute-start.30 = (s32[1,8,8]{2,1,0:T(8,128)}, s32[1,8,8]{2,1,0:T(8,128)S(1)}, u32[]{:S(2)}, u32[]{:S(2)}) collective-permute-start(s32[1,8,8]{2,1,0:T(8,128)} %param.15), channel_id=1, source_target_pairs={{0,64},{64,0},{1,65},{65,1},{2,66},{66,2},{3,67},{67,3},{4,68},{68... | collective-permute-start | bytes 776 | tf_op jit(solution)/shard_map/ppermute | solution.py:63
  4.2 5.0 %collective-permute-start.31 = (bf16[8,4736]{1,0:T(8,128)(2,1)S(1)}, bf16[8,4736]{1,0:T(8,128)(2,1)S(1)}, u32[]{:S(2)}, u32[]{:S(2)}) collective-permute-start(bf16[8,4736]{1,0:T(8,128)(2,1)S(1)} %concatenate.38), channel_id=1, source_target_pairs={{0,32},{1,33},{2,34},{3,35},{4,36},{5,37},{6,38},{7,39},{8,40},{9,... | collective-permute-start | bytes 227336 | tf_op jit(solution)/shard_map/ppermute | solution.py:43
  7.0 3.2 %collective-permute-start.32 = (bf16[8,4736]{1,0:T(8,128)(2,1)S(1)}, bf16[8,4736]{1,0:T(8,128)(2,1)S(1)}, u32[]{:S(2)}, u32[]{:S(2)}) collective-permute-start(bf16[8,4736]{1,0:T(8,128)(2,1)S(1)} %concatenate.38), channel_id=1, source_target_pairs={{0,48},{1,49},{2,50},{3,51},{4,52},{5,53},{6,54},{7,55},{8,56},{9,... | collective-permute-start | bytes 227336 | tf_op jit(solution)/shard_map/ppermute | solution.py:43
  7.9 4.4 %collective-permute-start.33 = (bf16[8,4736]{1,0:T(8,128)(2,1)S(1)}, bf16[8,4736]{1,0:T(8,128)(2,1)S(1)}, u32[]{:S(2)}, u32[]{:S(2)}) collective-permute-start(bf16[8,4736]{1,0:T(8,128)(2,1)S(1)} %concatenate.38), channel_id=1, source_target_pairs={{0,16},{1,17},{2,18},{3,19},{4,20},{5,21},{6,22},{7,23},{8,24},{9,... | collective-permute-start | bytes 227336 | tf_op jit(solution)/shard_map/ppermute | solution.py:43
  12.3 32.6 %copy-start.13 = (f32[1,512]{1,0:T(1,128)S(1)}, f32[1,512]{1,0:T(1,128)}, u32[]{:S(2)}) copy-start(f32[1,512]{1,0:T(1,128)} %refs_5_.1) | copy-start | bytes 6148
  12.3 8.2 %collective-permute-start.34 = (bf16[32,4736]{1,0:T(8,128)(2,1)S(1)}, bf16[32,4736]{1,0:T(8,128)(2,1)S(1)}, u32[]{:S(2)}, u32[]{:S(2)}) collective-permute-start(bf16[32,4736]{1,0:T(8,128)(2,1)S(1)} %pad_maximum_fusion.4.refs_0_), channel_id=1, source_target_pairs={{0,8},{1,9},{2,10},{3,11},{4,12},{5,13},{6,14},{7,15},{8,0},{9,1},... | collective-permute-start | bytes 909320 | tf_op jit(solution)/shard_map/ppermute | solution.py:43
  16.0 8.5 %collective-permute-start.35 = (bf16[32,4736]{1,0:T(8,128)(2,1)S(1)}, bf16[32,4736]{1,0:T(8,128)(2,1)S(1)}, u32[]{:S(2)}, u32[]{:S(2)}) collective-permute-start(bf16[32,4736]{1,0:T(8,128)(2,1)S(1)} %pad_maximum_fusion.4.refs_0_), channel_id=1, source_target_pairs={{0,12},{1,13},{2,14},{3,15},{4,0},{5,1},{6,2},{7,3},{8,4},{9,5},{1... | collective-permute-start | bytes 909320 | tf_op jit(solution)/shard_map/ppermute | solution.py:43
  16.4 8.1 %collective-permute-start.36 = (bf16[32,4736]{1,0:T(8,128)(2,1)S(1)}, bf16[32,4736]{1,0:T(8,128)(2,1)S(1)}, u32[]{:S(2)}, u32[]{:S(2)}) collective-permute-start(bf16[32,4736]{1,0:T(8,128)(2,1)S(1)} %pad_maximum_fusion.4.refs_0_), channel_id=1, source_target_pairs={{0,4},{1,5},{2,6},{3,7},{4,8},{5,9},{6,10},{7,11},{8,12},{9,13},{1... | collective-permute-start | bytes 909320 | tf_op jit(solution)/shard_map/ppermute | solution.py:43
  17.6 26.0 %copy-start = (bf16[512,2304]{1,0:T(8,128)(2,1)S(1)}, bf16[512,2304]{1,0:T(8,128)(2,1)}, u32[]{:S(2)}) copy-start(bf16[512,2304]{1,0:T(8,128)(2,1)} %cross_ref.3) | copy-start | bytes 7077892
  17.6 27.3 %copy-start.12 = (bf16[1,4608,512]{2,1,0:T(8,128)(2,1)S(1)}, bf16[1,4608,512]{2,1,0:T(8,128)(2,1)}, u32[]{:S(2)}) copy-start(bf16[1,4608,512]{2,1,0:T(8,128)(2,1)} %refs_4_.2) | copy-start | bytes 14155780
  24.5 27.2 %slice-start.2 = ((s8[4718592]{0:T(1024)(128)(4,1)}), s8[4194304]{0:T(1024)(128)(4,1)S(1)}, s32[]{:S(2)}) async-start(s8[4718592]{0:T(1024)(128)(4,1)} %bitcast.80), calls=%async_computation.2 | async-start | bytes 8388608
  26.2 10.8 %collective-permute-start.37 = (bf16[64,4736]{1,0:T(8,128)(2,1)S(1)}, bf16[64,4736]{1,0:T(8,128)(2,1)S(1)}, u32[]{:S(2)}, u32[]{:S(2)}) collective-permute-start(bf16[64,4736]{1,0:T(8,128)(2,1)S(1)} %get-tuple-element.127), channel_id=1, source_target_pairs={{0,2},{1,3},{2,0},{3,1},{4,6},{5,7},{6,4},{7,5},{8,10},{9,11},{10,... | collective-permute-start | bytes 1818632 | tf_op jit(solution)/shard_map/ppermute | solution.py:43
  28.9 14.7 %collective-permute-start.38 = (bf16[64,4736]{1,0:T(8,128)(2,1)S(1)}, bf16[64,4736]{1,0:T(8,128)(2,1)S(1)}, u32[]{:S(2)}, u32[]{:S(2)}) collective-permute-start(bf16[64,4736]{1,0:T(8,128)(2,1)S(1)} %get-tuple-element.128), channel_id=1, source_target_pairs={{0,3},{1,0},{2,1},{3,2},{4,7},{5,4},{6,5},{7,6},{8,11},{9,8},{10,9... | collective-permute-start | bytes 1818632 | tf_op jit(solution)/shard_map/ppermute | solution.py:43
  30.0 21.8 %slice-start.3 = ((s8[4718592]{0:T(1024)(128)(4,1)}), s8[524288]{0:T(1024)(128)(4,1)S(1)}, s32[]{:S(2)}) async-start(s8[4718592]{0:T(1024)(128)(4,1)} %bitcast.80), calls=%async_computation.3 | async-start | bytes 1048576
  30.0 13.6 %collective-permute-start.39 = (bf16[64,4736]{1,0:T(8,128)(2,1)S(1)}, bf16[64,4736]{1,0:T(8,128)(2,1)S(1)}, u32[]{:S(2)}, u32[]{:S(2)}) collective-permute-start(bf16[64,4736]{1,0:T(8,128)(2,1)S(1)} %get-tuple-element.129), channel_id=1, source_target_pairs={{0,1},{1,2},{2,3},{3,0},{4,5},{5,6},{6,7},{7,4},{8,9},{9,10},{10,1... | collective-permute-start | bytes 1818632 | tf_op jit(solution)/shard_map/ppermute | solution.py:43
  43.6 10.2 %collective-permute-start.41 = (bf16[512,2304]{1,0:T(8,128)(2,1)S(1)}, bf16[512,2304]{1,0:T(8,128)(2,1)S(1)}, u32[]{:S(2)}, u32[]{:S(2)}) collective-permute-start(bf16[512,2304]{1,0:T(8,128)(2,1)S(1)} %copy-done), channel_id=1, source_target_pairs={{0,64},{1,65},{2,66},{3,67},{4,68},{5,69},{6,70},{7,71},{8,72},{9,... | collective-permute-start | bytes 7077896 | tf_op jit(solution)/shard_map/ppermute | solution.py:55
  47.2 6.6 %collective-permute-start.40 = (bf16[256,640]{1,0:T(8,128)(2,1)S(1)}, bf16[256,640]{1,0:T(8,128)(2,1)S(1)}, u32[]{:S(2)}, u32[]{:S(2)}) collective-permute-start(bf16[256,640]{1,0:T(8,128)(2,1)S(1)} %get-tuple-element.135.codes_ref.own_ref), channel_id=1, source_target_pairs={{0,64},{64,0},{1,65},{65,1},{2,66},{66,2},{3,67},{67,3},{4,68},{68... | collective-permute-start | bytes 983048 | tf_op jit(solution)/shard_map/ppermute | solution.py:63
  53.8 76.2 %copy-start.2 = (bf16[512,2304]{1,0:T(8,128)(2,1)}, bf16[512,2304]{1,0:T(8,128)(2,1)S(1)}, u32[]{:S(2)}) copy-start(bf16[512,2304]{1,0:T(8,128)(2,1)S(1)} %collective-permute-done.41.cross_first_ref) | copy-start | bytes 7077892
  56.2 32.5 %copy-start.8 = (bf16[1,8,4608]{2,1,0:T(8,128)(2,1)S(1)}, bf16[1,8,4608]{2,1,0:T(8,128)(2,1)}, u32[]{:S(2)}) copy-start(bf16[1,8,4608]{2,1,0:T(8,128)(2,1)} %targets_ref.1) | copy-start | bytes 221188
  56.2 11.8 %collective-permute-start.42 = (bf16[64,5632]{1,0:T(8,128)(2,1)S(1)}, bf16[64,5632]{1,0:T(8,128)(2,1)S(1)}, u32[]{:S(2)}, u32[]{:S(2)}) collective-permute-start(bf16[64,5632]{1,0:T(8,128)(2,1)S(1)} %get-tuple-element.142), channel_id=1, source_target_pairs={{0,2},{1,3},{2,0},{3,1},{4,6},{5,7},{6,4},{7,5},{8,10},{9,11},{10,... | collective-permute-start | bytes 2162696 | tf_op jit(solution)/shard_map/ppermute | solution.py:43
  56.5 19.1 %collective-permute-start.43 = (bf16[64,5632]{1,0:T(8,128)(2,1)S(1)}, bf16[64,5632]{1,0:T(8,128)(2,1)S(1)}, u32[]{:S(2)}, u32[]{:S(2)}) collective-permute-start(bf16[64,5632]{1,0:T(8,128)(2,1)S(1)} %get-tuple-element.143), channel_id=1, source_target_pairs={{0,1},{1,2},{2,3},{3,0},{4,5},{5,6},{6,7},{7,4},{8,9},{9,10},{10,1... | collective-permute-start | bytes 2162696 | tf_op jit(solution)/shard_map/ppermute | solution.py:43
  56.6 19.0 %collective-permute-start.44 = (bf16[64,5632]{1,0:T(8,128)(2,1)S(1)}, bf16[64,5632]{1,0:T(8,128)(2,1)S(1)}, u32[]{:S(2)}, u32[]{:S(2)}) collective-permute-start(bf16[64,5632]{1,0:T(8,128)(2,1)S(1)} %get-tuple-element.144), channel_id=1, source_target_pairs={{0,3},{1,0},{2,1},{3,2},{4,7},{5,4},{6,5},{7,6},{8,11},{9,8},{10,9... | collective-permute-start | bytes 2162696 | tf_op jit(solution)/shard_map/ppermute | solution.py:43
  76.7 8.2 %collective-permute-start.45 = (bf16[32,5632]{1,0:T(8,128)(2,1)S(1)}, bf16[32,5632]{1,0:T(8,128)(2,1)S(1)}, u32[]{:S(2)}, u32[]{:S(2)}) collective-permute-start(bf16[32,5632]{1,0:T(8,128)(2,1)S(1)} %get-tuple-element.146), channel_id=1, source_target_pairs={{0,8},{1,9},{2,10},{3,11},{4,12},{5,13},{6,14},{7,15},{8,0},{9,1},... | collective-permute-start | bytes 1081352 | tf_op jit(solution)/shard_map/ppermute | solution.py:43
  79.0 9.7 %collective-permute-start.46 = (bf16[32,5632]{1,0:T(8,128)(2,1)S(1)}, bf16[32,5632]{1,0:T(8,128)(2,1)S(1)}, u32[]{:S(2)}, u32[]{:S(2)}) collective-permute-start(bf16[32,5632]{1,0:T(8,128)(2,1)S(1)} %get-tuple-element.147), channel_id=1, source_target_pairs={{0,4},{1,5},{2,6},{3,7},{4,8},{5,9},{6,10},{7,11},{8,12},{9,13},{1... | collective-permute-start | bytes 1081352 | tf_op jit(solution)/shard_map/ppermute | solution.py:43
  79.7 9.0 %collective-permute-start.47 = (bf16[32,5632]{1,0:T(8,128)(2,1)S(1)}, bf16[32,5632]{1,0:T(8,128)(2,1)S(1)}, u32[]{:S(2)}, u32[]{:S(2)}) collective-permute-start(bf16[32,5632]{1,0:T(8,128)(2,1)S(1)} %get-tuple-element.148), channel_id=1, source_target_pairs={{0,12},{1,13},{2,14},{3,15},{4,0},{5,1},{6,2},{7,3},{8,4},{9,5},{1... | collective-permute-start | bytes 1081352 | tf_op jit(solution)/shard_map/ppermute | solution.py:43
  89.5 7.6 %collective-permute-start.48 = (bf16[32,4864]{1,0:T(8,128)(2,1)S(1)}, bf16[32,4864]{1,0:T(8,128)(2,1)S(1)}, u32[]{:S(2)}, u32[]{:S(2)}) collective-permute-start(bf16[32,4864]{1,0:T(8,128)(2,1)S(1)} %get-tuple-element.150), channel_id=1, source_target_pairs={{0,32},{1,33},{2,34},{3,35},{4,36},{5,37},{6,38},{7,39},{8,40},{9,... | collective-permute-start | bytes 933896 | tf_op jit(solution)/shard_map/ppermute | solution.py:43
  91.6 8.3 %collective-permute-start.49 = (bf16[32,4864]{1,0:T(8,128)(2,1)S(1)}, bf16[32,4864]{1,0:T(8,128)(2,1)S(1)}, u32[]{:S(2)}, u32[]{:S(2)}) collective-permute-start(bf16[32,4864]{1,0:T(8,128)(2,1)S(1)} %get-tuple-element.151), channel_id=1, source_target_pairs={{0,48},{1,49},{2,50},{3,51},{4,52},{5,53},{6,54},{7,55},{8,56},{9,... | collective-permute-start | bytes 933896 | tf_op jit(solution)/shard_map/ppermute | solution.py:43
  92.6 7.9 %collective-permute-start.50 = (bf16[32,4864]{1,0:T(8,128)(2,1)S(1)}, bf16[32,4864]{1,0:T(8,128)(2,1)S(1)}, u32[]{:S(2)}, u32[]{:S(2)}) collective-permute-start(bf16[32,4864]{1,0:T(8,128)(2,1)S(1)} %get-tuple-element.152), channel_id=1, source_target_pairs={{0,16},{1,17},{2,18},{3,19},{4,20},{5,21},{6,22},{7,23},{8,24},{9,... | collective-permute-start | bytes 933896 | tf_op jit(solution)/shard_map/ppermute | solution.py:43
  101.1 7.5 %collective-permute-start.51 = (bf16[32,4608]{1,0:T(8,128)(2,1)S(1)}, bf16[32,4608]{1,0:T(8,128)(2,1)S(1)}, u32[]{:S(2)}, u32[]{:S(2)}) collective-permute-start(bf16[32,4608]{1,0:T(8,128)(2,1)S(1)} %get-tuple-element.153.refs_0_), channel_id=1, source_target_pairs={{0,8},{1,9},{2,10},{3,11},{4,12},{5,13},{6,14},{7,15},{8,0},{9,1},... | collective-permute-start | bytes 884744 | tf_op jit(solution)/shard_map/ppermute | solution.py:43
  102.9 8.8 %collective-permute-start.52 = (bf16[32,4608]{1,0:T(8,128)(2,1)S(1)}, bf16[32,4608]{1,0:T(8,128)(2,1)S(1)}, u32[]{:S(2)}, u32[]{:S(2)}) collective-permute-start(bf16[32,4608]{1,0:T(8,128)(2,1)S(1)} %get-tuple-element.153.refs_0_), channel_id=1, source_target_pairs={{0,12},{1,13},{2,14},{3,15},{4,0},{5,1},{6,2},{7,3},{8,4},{9,5},{1... | collective-permute-start | bytes 884744 | tf_op jit(solution)/shard_map/ppermute | solution.py:43
  104.3 7.4 %collective-permute-start.53 = (bf16[32,4608]{1,0:T(8,128)(2,1)S(1)}, bf16[32,4608]{1,0:T(8,128)(2,1)S(1)}, u32[]{:S(2)}, u32[]{:S(2)}) collective-permute-start(bf16[32,4608]{1,0:T(8,128)(2,1)S(1)} %get-tuple-element.153.refs_0_), channel_id=1, source_target_pairs={{0,4},{1,5},{2,6},{3,7},{4,8},{5,9},{6,10},{7,11},{8,12},{9,13},{1... | collective-permute-start | bytes 884744 | tf_op jit(solution)/shard_map/ppermute | solution.py:43
  113.0 10.7 %collective-permute-start.54 = (bf16[64,4608]{1,0:T(8,128)(2,1)S(1)}, bf16[64,4608]{1,0:T(8,128)(2,1)S(1)}, u32[]{:S(2)}, u32[]{:S(2)}) collective-permute-start(bf16[64,4608]{1,0:T(8,128)(2,1)S(1)} %get-tuple-element.155), channel_id=1, source_target_pairs={{0,2},{1,3},{2,0},{3,1},{4,6},{5,7},{6,4},{7,5},{8,10},{9,11},{10,... | collective-permute-start | bytes 1769480 | tf_op jit(solution)/shard_map/ppermute | solution.py:43
  113.1 14.9 %collective-permute-start.55 = (bf16[64,4608]{1,0:T(8,128)(2,1)S(1)}, bf16[64,4608]{1,0:T(8,128)(2,1)S(1)}, u32[]{:S(2)}, u32[]{:S(2)}) collective-permute-start(bf16[64,4608]{1,0:T(8,128)(2,1)S(1)} %get-tuple-element.156), channel_id=1, source_target_pairs={{0,3},{1,0},{2,1},{3,2},{4,7},{5,4},{6,5},{7,6},{8,11},{9,8},{10,9... | collective-permute-start | bytes 1769480 | tf_op jit(solution)/shard_map/ppermute | solution.py:43
  114.8 15.2 %collective-permute-start.56 = (bf16[64,4608]{1,0:T(8,128)(2,1)S(1)}, bf16[64,4608]{1,0:T(8,128)(2,1)S(1)}, u32[]{:S(2)}, u32[]{:S(2)}) collective-permute-start(bf16[64,4608]{1,0:T(8,128)(2,1)S(1)} %get-tuple-element.157), channel_id=1, source_target_pairs={{0,1},{1,2},{2,3},{3,0},{4,5},{5,6},{6,7},{7,4},{8,9},{9,10},{10,1... | collective-permute-start | bytes 1769480 | tf_op jit(solution)/shard_map/ppermute | solution.py:43
  132.2 8.0 %collective-permute-start.57 = (bf16[256,3328]{1,0:T(8,128)(2,1)S(1)}, bf16[256,3328]{1,0:T(8,128)(2,1)S(1)}, u32[]{:S(2)}, u32[]{:S(2)}) collective-permute-start(bf16[256,3328]{1,0:T(8,128)(2,1)S(1)} %cross_back.1), channel_id=1, source_target_pairs={{64,0},{65,1},{66,2},{67,3},{68,4},{69,5},{70,6},{71,7},{72,8},{73... | collective-permute-start | bytes 5111816 | tf_op jit(solution)/shard_map/ppermute | solution.py:59
  140.2 4.7 %copy-start.7 = (bf16[1,8,4608]{2,1,0:T(8,128)(2,1)S(1)}, bf16[1,8,4608]{2,1,0:T(8,128)(2,1)}, u32[]{:S(2)}) copy-start(bf16[1,8,4608]{2,1,0:T(8,128)(2,1)} %param.9) | copy-start | bytes 221188
  140.2 4.7 %copy-start.11 = (s32[1,8,8]{2,1,0:T(8,128)S(1)}, s32[1,8,8]{2,1,0:T(8,128)}, u32[]{:S(2)}) copy-start(s32[1,8,8]{2,1,0:T(8,128)} %param.15) | copy-start | bytes 772

commit v2 on v1

--- a/solution.py
+++ b/solution.py
@@ -13,7 +13,7 @@
 PLANE = 128
 CAP = 64
 ROWS = SIDE * CAP
-AWAY = (0, 2, 1, 3)
+AWAY = (0, 2, 3, 1)
 STEPS = {"y": (1, 0, 0), "x": (0, 1, 0), "z": (0, 0, 1)}
 F32, BF16 = jnp.float32, jnp.bfloat16
 

time: 146 us -> 145 us (level)
  waiting for transfers between devices: 77.6 us -> 71.3 us
  starting transfers between devices: 41.7 us -> 46.9 us
    ppermute x24, starting transfers between devices: 30.2 us -> 36.6 us  [send(): return lax.ppermute(block, ('layer', 'feat'), route(axes, distance))]
    ppermute x24, waiting for transfers between devices: 77.3 us -> 71 us  [send(): return lax.ppermute(block, ('layer', 'feat'), route(axes, distance))]
  transfers between devices with their start and end apart: 28 -> 28, of which waited for: 20 -> 18; matrix products, arithmetic and copies ran while one was open for 1% -> 1% of each run, Pallas kernels for 6% -> 6%
where the time goes in v2:
time: 145 us
  waiting for transfers between devices  71.3 us (49%)
  starting transfers between devices  46.9 us (32%)
  Pallas kernels  22.9 us (16%)
    ppermute x24, waiting for transfers between devices, send(): return lax.ppermute(block, ('layer', 'feat'), route(axes, distance))  71 us
    ppermute x24, starting transfers between devices, send(): return lax.ppermute(block, ('layer', 'feat'), route(axes, distance))  36.6 us
    pallas_call x11, Pallas kernels, call(): pl.pallas_call(kernel, in_specs=[smem] + [vmem] * len(ins), out_specs=[pl...  22.9 us
    ppermute x2, starting transfers between devices, swapped(): return lax.ppermute(block, 'layer', [(0, 1), (1, 0)])  5.13 us
    ppermute x1, starting transfers between devices, to_first(): return lax.ppermute(block, 'layer', [(1, 0)])  3.89 us
  transfers between devices with their start and end apart: 28, of which 18 were waited for; matrix products, arithmetic and copies ran while one was open for 1% of the time, Pallas kernels for 6%

profile of v2, /device:TPU:1, one launch (start us, length us, event | category | flops | bytes accessed | tf_op | source)
XLA Modules:
  0.0 144.9 jit_solution(7249805433904823978)
XLA Ops:
  0.6 1.5 %collective-permute-start.30 = (s32[1,8,8]{2,1,0:T(8,128)}, s32[1,8,8]{2,1,0:T(8,128)S(1)}, u32[]{:S(2)}, u32[]{:S(2)}) collective-permute-start(s32[1,8,8]{2,1,0:T(8,128)} %param.15), channel_id=1, source_target_pairs={{0,64},{64,0},{1,65},{65,1},{2,66},{66,2},{3,67},{67,3},{4,68},{68... | collective-permute-start | bytes 776 | tf_op jit(solution)/shard_map/ppermute | solution.py:63
  3.2 1.0 concatenate.38
  4.2 2.8 %collective-permute-start.31 = (bf16[8,4736]{1,0:T(8,128)(2,1)S(1)}, bf16[8,4736]{1,0:T(8,128)(2,1)S(1)}, u32[]{:S(2)}, u32[]{:S(2)}) collective-permute-start(bf16[8,4736]{1,0:T(8,128)(2,1)S(1)} %concatenate.38), channel_id=1, source_target_pairs={{0,32},{1,33},{2,34},{3,35},{4,36},{5,37},{6,38},{7,39},{8,40},{9,... | collective-permute-start | bytes 227336 | tf_op jit(solution)/shard_map/ppermute | solution.py:43
  7.3 2.4 %collective-permute-start.33 = (bf16[8,4736]{1,0:T(8,128)(2,1)S(1)}, bf16[8,4736]{1,0:T(8,128)(2,1)S(1)}, u32[]{:S(2)}, u32[]{:S(2)}) collective-permute-start(bf16[8,4736]{1,0:T(8,128)(2,1)S(1)} %concatenate.38), channel_id=1, source_target_pairs={{0,48},{1,49},{2,50},{3,51},{4,52},{5,53},{6,54},{7,55},{8,56},{9,... | collective-permute-start | bytes 227336 | tf_op jit(solution)/shard_map/ppermute | solution.py:43
  9.7 1.8 %collective-permute-done.32 = bf16[8,4736]{1,0:T(8,128)(2,1)S(1)} collective-permute-done((bf16[8,4736]{1,0:T(8,128)(2,1)S(1)}, bf16[8,4736]{1,0:T(8,128)(2,1)S(1)}, u32[]{:S(2)}, u32[]{:S(2)}) %collective-permute-start.32) | collective-permute-done | bytes 75808 | tf_op jit(solution)/shard_map/ppermute | solution.py:43
  11.5 3.7 %collective-permute-start.34 = (bf16[32,4736]{1,0:T(8,128)(2,1)S(1)}, bf16[32,4736]{1,0:T(8,128)(2,1)S(1)}, u32[]{:S(2)}, u32[]{:S(2)}) collective-permute-start(bf16[32,4736]{1,0:T(8,128)(2,1)S(1)} %pad_maximum_fusion.4.refs_0_), channel_id=1, source_target_pairs={{0,8},{1,9},{2,10},{3,11},{4,12},{5,13},{6,14},{7,15},{8,0},{9,1},... | collective-permute-start | bytes 909320 | tf_op jit(solution)/shard_map/ppermute | solution.py:43
  15.1 0.7 collective-permute-start.35
  15.9 1.9 %collective-permute-start.36 = (bf16[32,4736]{1,0:T(8,128)(2,1)S(1)}, bf16[32,4736]{1,0:T(8,128)(2,1)S(1)}, u32[]{:S(2)}, u32[]{:S(2)}) collective-permute-start(bf16[32,4736]{1,0:T(8,128)(2,1)S(1)} %pad_maximum_fusion.4.refs_0_), channel_id=1, source_target_pairs={{0,12},{1,13},{2,14},{3,15},{4,0},{5,1},{6,2},{7,3},{8,4},{9,5},{1... | collective-permute-start | bytes 909320 | tf_op jit(solution)/shard_map/ppermute | solution.py:43
  17.9 1.7 %collective-permute-done.34.refs_1_ = bf16[32,4736]{1,0:T(8,128)(2,1)S(1)} collective-permute-done((bf16[32,4736]{1,0:T(8,128)(2,1)S(1)}, bf16[32,4736]{1,0:T(8,128)(2,1)S(1)}, u32[]{:S(2)}, u32[]{:S(2)}) %collective-permute-start.34) | collective-permute-done | bytes 303136 | tf_op jit(solution)/shard_map/ppermute | solution.py:43
  19.6 3.2 %collective-permute-done.35.refs_2_ = bf16[32,4736]{1,0:T(8,128)(2,1)S(1)} collective-permute-done((bf16[32,4736]{1,0:T(8,128)(2,1)S(1)}, bf16[32,4736]{1,0:T(8,128)(2,1)S(1)}, u32[]{:S(2)}, u32[]{:S(2)}) %collective-permute-start.35) | collective-permute-done | bytes 303136 | tf_op jit(solution)/shard_map/ppermute | solution.py:43
  23.6 1.7 %select.26 = (bf16[64,4736]{1,0:T(8,128)(2,1)S(1)}, bf16[64,4736]{1,0:T(8,128)(2,1)S(1)}, bf16[64,4736]{1,0:T(8,128)(2,1)S(1)}, bf16[64,4736]{1,0:T(8,128)(2,1)S...) custom-call(s32[6]{0:T(128)S(1)} %stack.27.s, ...), custom_call_target="tpu_custom_call" | custom-call | flops 2147483648 | bytes 1212416 | tf_op jit(solution)/shard_map/select/pallas_call | solution.py:90
  25.3 2.7 %collective-permute-start.37 = (bf16[64,4736]{1,0:T(8,128)(2,1)S(1)}, bf16[64,4736]{1,0:T(8,128)(2,1)S(1)}, u32[]{:S(2)}, u32[]{:S(2)}) collective-permute-start(bf16[64,4736]{1,0:T(8,128)(2,1)S(1)} %get-tuple-element.127), channel_id=1, source_target_pairs={{0,2},{1,3},{2,0},{3,1},{4,6},{5,7},{6,4},{7,5},{8,10},{9,11},{10,... | collective-permute-start | bytes 1818632 | tf_op jit(solution)/shard_map/ppermute | solution.py:43
  28.7 2.0 %collective-permute-start.39 = (bf16[64,4736]{1,0:T(8,128)(2,1)S(1)}, bf16[64,4736]{1,0:T(8,128)(2,1)S(1)}, u32[]{:S(2)}, u32[]{:S(2)}) collective-permute-start(bf16[64,4736]{1,0:T(8,128)(2,1)S(1)} %get-tuple-element.129), channel_id=1, source_target_pairs={{0,3},{1,0},{2,1},{3,2},{4,7},{5,4},{6,5},{7,6},{8,11},{9,8},{10,9... | collective-permute-start | bytes 1818632 | tf_op jit(solution)/shard_map/ppermute | solution.py:43
  30.7 5.4 %collective-permute-done.37.refs_1_ = bf16[64,4736]{1,0:T(8,128)(2,1)S(1)} collective-permute-done((bf16[64,4736]{1,0:T(8,128)(2,1)S(1)}, bf16[64,4736]{1,0:T(8,128)(2,1)S(1)}, u32[]{:S(2)}, u32[]{:S(2)}) %collective-permute-start.37) | collective-permute-done | bytes 606240 | tf_op jit(solution)/shard_map/ppermute | solution.py:43
  36.1 6.5 %collective-permute-done.38.refs_2_ = bf16[64,4736]{1,0:T(8,128)(2,1)S(1)} collective-permute-done((bf16[64,4736]{1,0:T(8,128)(2,1)S(1)}, bf16[64,4736]{1,0:T(8,128)(2,1)S(1)}, u32[]{:S(2)}, u32[]{:S(2)}) %collective-permute-start.38) | collective-permute-done | bytes 606240 | tf_op jit(solution)/shard_map/ppermute | solution.py:43
  43.0 1.3 collective-permute-start.41
  44.3 2.3 %encode.1 = (bf16[256,640]{1,0:T(8,128)(2,1)S(1)}, f32[256,512]{1,0:T(8,128)S(1)}) custom-call(s32[6]{0:T(128)S(1)} %stack.27.s, bf16[64,4736]{1,0:T(8,128)(2,1)S(1)} %get-tuple-element.130.refs_0_, bf16[64,4736]{1,0:T(8,128)(2,1)S(1)} %collective-permute-done.37.refs_1_, bf16[64,4736]{1,0:T(8,128)(2,1)S(1)} %collective-permute-done.38.refs_2_, ...), custom_call_target="tpu_custom_call" | custom-call | flops 2147483648 | bytes 7161856 | tf_op jit(solution)/shard_map/encode/pallas_call | solution.py:90
  46.5 3.6 %collective-permute-start.40 = (bf16[256,640]{1,0:T(8,128)(2,1)S(1)}, bf16[256,640]{1,0:T(8,128)(2,1)S(1)}, u32[]{:S(2)}, u32[]{:S(2)}) collective-permute-start(bf16[256,640]{1,0:T(8,128)(2,1)S(1)} %get-tuple-element.135.codes_ref.own_ref), channel_id=1, source_target_pairs={{0,64},{64,0},{1,65},{65,1},{2,66},{66,2},{3,67},{67,3},{4,68},{68... | collective-permute-start | bytes 983048 | tf_op jit(solution)/shard_map/ppermute | solution.py:63
  50.2 2.0 %decode_self.1 = (f32[256,4608]{1,0:T(8,128)S(1)}, bf16[256,1024]{1,0:T(8,128)(2,1)S(1)}) custom-call(s32[6]{0:T(128)S(1)} %stack.27.s, bf16[256,640]{1,0:T(8,128)(2,1)S(1)} %get-tuple-element.135.codes_ref.own_ref, bf16[1,512,4608]{2,1,0:T(8,128)(2,1)S(1)} %bitcast.81), custom_call_target="tpu_custom_call" | custom-call | flops 2147483648 | bytes 5046272 | tf_op jit(solution)/shard_map/decode_self/pallas_call | solution.py:90
  52.2 2.4 %decode.1 = (bf16[64,5632]{1,0:T(8,128)(2,1)S(1)}, bf16[64,5632]{1,0:T(8,128)(2,1)S(1)}, bf16[64,5632]{1,0:T(8,128)(2,1)S(1)}, bf16[64,5632]{1,0:T(8,128)(2,1)S(...) custom-call(s32[6]{0:T(128)S(1)} %stack.27.s, bf16[256,640]{1,0:T(8,128)(2,1)S(1)} %get-tuple-element.135.codes_ref.own_ref, ...), custom_call_target="tpu_custom_call" | custom-call | flops 2147483648 | bytes 10616832 | tf_op jit(solution)/shard_map/decode/pallas_call | solution.py:90
  54.6 1.3 collective-permute-start.42
  55.9 1.8 %collective-permute-start.43 = (bf16[64,5632]{1,0:T(8,128)(2,1)S(1)}, bf16[64,5632]{1,0:T(8,128)(2,1)S(1)}, u32[]{:S(2)}, u32[]{:S(2)}) collective-permute-start(bf16[64,5632]{1,0:T(8,128)(2,1)S(1)} %get-tuple-element.143), channel_id=1, source_target_pairs={{0,3},{1,0},{2,1},{3,2},{4,7},{5,4},{6,5},{7,6},{8,11},{9,8},{10,9... | collective-permute-start | bytes 2162696 | tf_op jit(solution)/shard_map/ppermute | solution.py:43
  58.2 8.2 %collective-permute-done.42.refs_1_ = bf16[64,5632]{1,0:T(8,128)(2,1)S(1)} collective-permute-done((bf16[64,5632]{1,0:T(8,128)(2,1)S(1)}, bf16[64,5632]{1,0:T(8,128)(2,1)S(1)}, u32[]{:S(2)}, u32[]{:S(2)}) %collective-permute-start.42) | collective-permute-done | bytes 720928 | tf_op jit(solution)/shard_map/ppermute | solution.py:43
  66.5 8.2 %collective-permute-done.43.refs_2_ = bf16[64,5632]{1,0:T(8,128)(2,1)S(1)} collective-permute-done((bf16[64,5632]{1,0:T(8,128)(2,1)S(1)}, bf16[64,5632]{1,0:T(8,128)(2,1)S(1)}, u32[]{:S(2)}, u32[]{:S(2)}) %collective-permute-start.43) | collective-permute-done | bytes 720928 | tf_op jit(solution)/shard_map/ppermute | solution.py:43
  74.7 1.1 spread.1
  75.8 1.8 %collective-permute-start.45 = (bf16[32,5632]{1,0:T(8,128)(2,1)S(1)}, bf16[32,5632]{1,0:T(8,128)(2,1)S(1)}, u32[]{:S(2)}, u32[]{:S(2)}) collective-permute-start(bf16[32,5632]{1,0:T(8,128)(2,1)S(1)} %get-tuple-element.146), channel_id=1, source_target_pairs={{0,8},{1,9},{2,10},{3,11},{4,12},{5,13},{6,14},{7,15},{8,0},{9,1},... | collective-permute-start | bytes 1081352 | tf_op jit(solution)/shard_map/ppermute | solution.py:43
  77.6 1.4 collective-permute-start.46
  79.1 4.8 %collective-permute-done.45.refs_1_ = bf16[32,5632]{1,0:T(8,128)(2,1)S(1)} collective-permute-done((bf16[32,5632]{1,0:T(8,128)(2,1)S(1)}, bf16[32,5632]{1,0:T(8,128)(2,1)S(1)}, u32[]{:S(2)}, u32[]{:S(2)}) %collective-permute-start.45) | collective-permute-done | bytes 360480 | tf_op jit(solution)/shard_map/ppermute | solution.py:43
  83.9 3.9 %collective-permute-done.46.refs_2_ = bf16[32,5632]{1,0:T(8,128)(2,1)S(1)} collective-permute-done((bf16[32,5632]{1,0:T(8,128)(2,1)S(1)}, bf16[32,5632]{1,0:T(8,128)(2,1)S(1)}, u32[]{:S(2)}, u32[]{:S(2)}) %collective-permute-start.46) | collective-permute-done | bytes 360480 | tf_op jit(solution)/shard_map/ppermute | solution.py:43
  88.5 1.9 %collective-permute-start.48 = (bf16[32,4864]{1,0:T(8,128)(2,1)S(1)}, bf16[32,4864]{1,0:T(8,128)(2,1)S(1)}, u32[]{:S(2)}, u32[]{:S(2)}) collective-permute-start(bf16[32,4864]{1,0:T(8,128)(2,1)S(1)} %get-tuple-element.150), channel_id=1, source_target_pairs={{0,32},{1,33},{2,34},{3,35},{4,36},{5,37},{6,38},{7,39},{8,40},{9,... | collective-permute-start | bytes 933896 | tf_op jit(solution)/shard_map/ppermute | solution.py:43
  90.4 1.1 collective-permute-start.49
  91.6 1.6 %collective-permute-start.50 = (bf16[32,4864]{1,0:T(8,128)(2,1)S(1)}, bf16[32,4864]{1,0:T(8,128)(2,1)S(1)}, u32[]{:S(2)}, u32[]{:S(2)}) collective-permute-start(bf16[32,4864]{1,0:T(8,128)(2,1)S(1)} %get-tuple-element.152), channel_id=1, source_target_pairs={{0,48},{1,49},{2,50},{3,51},{4,52},{5,53},{6,54},{7,55},{8,56},{9,... | collective-permute-start | bytes 933896 | tf_op jit(solution)/shard_map/ppermute | solution.py:43
  93.1 3.1 %collective-permute-done.48.refs_0_ = bf16[32,4864]{1,0:T(8,128)(2,1)S(1)} collective-permute-done((bf16[32,4864]{1,0:T(8,128)(2,1)S(1)}, bf16[32,4864]{1,0:T(8,128)(2,1)S(1)}, u32[]{:S(2)}, u32[]{:S(2)}) %collective-permute-start.48) | collective-permute-done | bytes 311328 | tf_op jit(solution)/shard_map/ppermute | solution.py:43
  96.2 3.3 %collective-permute-done.49.refs_1_ = bf16[32,4864]{1,0:T(8,128)(2,1)S(1)} collective-permute-done((bf16[32,4864]{1,0:T(8,128)(2,1)S(1)}, bf16[32,4864]{1,0:T(8,128)(2,1)S(1)}, u32[]{:S(2)}, u32[]{:S(2)}) %collective-permute-start.49) | collective-permute-done | bytes 311328 | tf_op jit(solution)/shard_map/ppermute | solution.py:43
  100.2 1.8 %collective-permute-start.51 = (bf16[32,4608]{1,0:T(8,128)(2,1)S(1)}, bf16[32,4608]{1,0:T(8,128)(2,1)S(1)}, u32[]{:S(2)}, u32[]{:S(2)}) collective-permute-start(bf16[32,4608]{1,0:T(8,128)(2,1)S(1)} %get-tuple-element.153.refs_0_), channel_id=1, source_target_pairs={{0,8},{1,9},{2,10},{3,11},{4,12},{5,13},{6,14},{7,15},{8,0},{9,1},... | collective-permute-start | bytes 884744 | tf_op jit(solution)/shard_map/ppermute | solution.py:43
  102.0 1.2 collective-permute-start.52
  103.2 1.5 %collective-permute-start.53 = (bf16[32,4608]{1,0:T(8,128)(2,1)S(1)}, bf16[32,4608]{1,0:T(8,128)(2,1)S(1)}, u32[]{:S(2)}, u32[]{:S(2)}) collective-permute-start(bf16[32,4608]{1,0:T(8,128)(2,1)S(1)} %get-tuple-element.153.refs_0_), channel_id=1, source_target_pairs={{0,12},{1,13},{2,14},{3,15},{4,0},{5,1},{6,2},{7,3},{8,4},{9,5},{1... | collective-permute-start | bytes 884744 | tf_op jit(solution)/shard_map/ppermute | solution.py:43
  104.7 3.0 %collective-permute-done.51.refs_1_ = bf16[32,4608]{1,0:T(8,128)(2,1)S(1)} collective-permute-done((bf16[32,4608]{1,0:T(8,128)(2,1)S(1)}, bf16[32,4608]{1,0:T(8,128)(2,1)S(1)}, u32[]{:S(2)}, u32[]{:S(2)}) %collective-permute-start.51) | collective-permute-done | bytes 294944 | tf_op jit(solution)/shard_map/ppermute | solution.py:43
  107.7 3.1 %collective-permute-done.52.refs_2_ = bf16[32,4608]{1,0:T(8,128)(2,1)S(1)} collective-permute-done((bf16[32,4608]{1,0:T(8,128)(2,1)S(1)}, bf16[32,4608]{1,0:T(8,128)(2,1)S(1)}, u32[]{:S(2)}, u32[]{:S(2)}) %collective-permute-start.52) | collective-permute-done | bytes 294944 | tf_op jit(solution)/shard_map/ppermute | solution.py:43
  110.8 1.3 compact.1
  112.8 2.1 %collective-permute-start.55 = (bf16[64,4608]{1,0:T(8,128)(2,1)S(1)}, bf16[64,4608]{1,0:T(8,128)(2,1)S(1)}, u32[]{:S(2)}, u32[]{:S(2)}) collective-permute-start(bf16[64,4608]{1,0:T(8,128)(2,1)S(1)} %get-tuple-element.156), channel_id=1, source_target_pairs={{0,1},{1,2},{2,3},{3,0},{4,5},{5,6},{6,7},{7,4},{8,9},{9,10},{10,1... | collective-permute-start | bytes 1769480 | tf_op jit(solution)/shard_map/ppermute | solution.py:43
  115.5 7.3 %collective-permute-done.54.refs_1_.refs_5_ = bf16[64,4608]{1,0:T(8,128)(2,1)S(1)} collective-permute-done((bf16[64,4608]{1,0:T(8,128)(2,1)S(1)}, bf16[64,4608]{1,0:T(8,128)(2,1)S(1)}, u32[]{:S(2)}, u32[]{:S(2)}) %collective-permute-start.54) | collective-permute-done | bytes 589856 | tf_op jit(solution)/shard_map/ppermute | solution.py:43
  122.8 6.3 %collective-permute-done.55.refs_2_.refs_6_ = bf16[64,4608]{1,0:T(8,128)(2,1)S(1)} collective-permute-done((bf16[64,4608]{1,0:T(8,128)(2,1)S(1)}, bf16[64,4608]{1,0:T(8,128)(2,1)S(1)}, u32[]{:S(2)}, u32[]{:S(2)}) %collective-permute-start.55) | collective-permute-done | bytes 589856 | tf_op jit(solution)/shard_map/ppermute | solution.py:43
  129.1 2.2 %cross_back.1 = bf16[256,3328]{1,0:T(8,128)(2,1)S(1)} custom-call(s32[6]{0:T(128)S(1)} %stack.27.s, bf16[256,256]{1,0:T(8,128)(2,1)S(1)} %get-tuple-element.161.match_ref, bf16[512,2304]{1,0:T(8,128)(2,1)S(1)} %collective-permute-done.41.cross_first_ref, bf16[512,2304]{1,0:T(8,128)(2,1)S(1)} %copy-done, ...), custom_call_target="tpu_custom_call" | custom-call | flops 2147483648 | bytes 7208960 | tf_op jit(solution)/shard_map/cross_back/pallas_call | solution.py:90
  131.3 3.9 %collective-permute-start.57 = (bf16[256,3328]{1,0:T(8,128)(2,1)S(1)}, bf16[256,3328]{1,0:T(8,128)(2,1)S(1)}, u32[]{:S(2)}, u32[]{:S(2)}) collective-permute-start(bf16[256,3328]{1,0:T(8,128)(2,1)S(1)} %cross_back.1), channel_id=1, source_target_pairs={{64,0},{65,1},{66,2},{67,3},{68,4},{69,5},{70,6},{71,7},{72,8},{73... | collective-permute-start | bytes 5111816 | tf_op jit(solution)/shard_map/ppermute | solution.py:59
  135.2 3.9 %self_back.1 = (f32[256,512]{1,0:T(8,128)S(1)}, bf16[1,512,4608]{2,1,0:T(8,128)(2,1)}) custom-call(s32[6]{0:T(128)S(1)} %stack.27.s, bf16[256,640]{1,0:T(8,128)(2,1)S(1)} %get-tuple-element.135.codes_ref.own_ref, bf16[1,512,4608]{2,1,0:T(8,128)(2,1)S(1)} %bitcast.81, bf16[64,4608]{1,0:T(8,128)(2,1)S(1)} %get-tuple-element.154.refs_0_.refs_4_, ...), custom_call_target="tpu_custom_call" | custom-call | flops 2147483648 | bytes 7405568 | tf_op jit(solution)/shard_map/self_back/pallas_call | solution.py:90
  139.1 4.7 %last.1 = (bf16[1,4608,512]{2,1,0:T(8,128)(2,1)}, f32[1,512]{1,0:T(1,128)}, bf16[512,2304]{1,0:T(8,128)(2,1)}, bf16[64,128]{1,0:T(8,128)(2,1)}, f32[1,8,4608]{2,1,0:T(8,128)}, /*index=5*/s32[1]{0:T(128)}) custom-call(s32[6]{0:T(128)S(1)} %stack.27.s, f32[256,512]{1,0:T(8,128)S(1)} %get-tuple-element.158.term_ref, ...), custom_call_target="tpu_custom_call" | custom-call | flops 2147483648 | bytes 8052736 | tf_op jit(solution)/shard_map/last/pallas_call | solution.py:90
  143.8 0.9 while.19
  (47 shorter events, 6.6 us)
Async XLA Ops:
  0.6 2.5 %collective-permute-start.30 = (s32[1,8,8]{2,1,0:T(8,128)}, s32[1,8,8]{2,1,0:T(8,128)S(1)}, u32[]{:S(2)}, u32[]{:S(2)}) collective-permute-start(s32[1,8,8]{2,1,0:T(8,128)} %param.15), channel_id=1, source_target_pairs={{0,64},{64,0},{1,65},{65,1},{2,66},{66,2},{3,67},{67,3},{4,68},{68... | collective-permute-start | bytes 776 | tf_op jit(solution)/shard_map/ppermute | solution.py:63
  4.2 5.5 %collective-permute-start.31 = (bf16[8,4736]{1,0:T(8,128)(2,1)S(1)}, bf16[8,4736]{1,0:T(8,128)(2,1)S(1)}, u32[]{:S(2)}, u32[]{:S(2)}) collective-permute-start(bf16[8,4736]{1,0:T(8,128)(2,1)S(1)} %concatenate.38), channel_id=1, source_target_pairs={{0,32},{1,33},{2,34},{3,35},{4,36},{5,37},{6,38},{7,39},{8,40},{9,... | collective-permute-start | bytes 227336 | tf_op jit(solution)/shard_map/ppermute | solution.py:43
  7.0 4.4 %collective-permute-start.32 = (bf16[8,4736]{1,0:T(8,128)(2,1)S(1)}, bf16[8,4736]{1,0:T(8,128)(2,1)S(1)}, u32[]{:S(2)}, u32[]{:S(2)}) collective-permute-start(bf16[8,4736]{1,0:T(8,128)(2,1)S(1)} %concatenate.38), channel_id=1, source_target_pairs={{0,16},{1,17},{2,18},{3,19},{4,20},{5,21},{6,22},{7,23},{8,24},{9,... | collective-permute-start | bytes 227336 | tf_op jit(solution)/shard_map/ppermute | solution.py:43
  7.3 4.1 %collective-permute-start.33 = (bf16[8,4736]{1,0:T(8,128)(2,1)S(1)}, bf16[8,4736]{1,0:T(8,128)(2,1)S(1)}, u32[]{:S(2)}, u32[]{:S(2)}) collective-permute-start(bf16[8,4736]{1,0:T(8,128)(2,1)S(1)} %concatenate.38), channel_id=1, source_target_pairs={{0,48},{1,49},{2,50},{3,51},{4,52},{5,53},{6,54},{7,55},{8,56},{9,... | collective-permute-start | bytes 227336 | tf_op jit(solution)/shard_map/ppermute | solution.py:43
  11.5 32.8 %copy-start.13 = (f32[1,512]{1,0:T(1,128)S(1)}, f32[1,512]{1,0:T(1,128)}, u32[]{:S(2)}) copy-start(f32[1,512]{1,0:T(1,128)} %refs_5_.1) | copy-start | bytes 6148
  11.5 8.2 %collective-permute-start.34 = (bf16[32,4736]{1,0:T(8,128)(2,1)S(1)}, bf16[32,4736]{1,0:T(8,128)(2,1)S(1)}, u32[]{:S(2)}, u32[]{:S(2)}) collective-permute-start(bf16[32,4736]{1,0:T(8,128)(2,1)S(1)} %pad_maximum_fusion.4.refs_0_), channel_id=1, source_target_pairs={{0,8},{1,9},{2,10},{3,11},{4,12},{5,13},{6,14},{7,15},{8,0},{9,1},... | collective-permute-start | bytes 909320 | tf_op jit(solution)/shard_map/ppermute | solution.py:43
  15.1 7.7 %collective-permute-start.35 = (bf16[32,4736]{1,0:T(8,128)(2,1)S(1)}, bf16[32,4736]{1,0:T(8,128)(2,1)S(1)}, u32[]{:S(2)}, u32[]{:S(2)}) collective-permute-start(bf16[32,4736]{1,0:T(8,128)(2,1)S(1)} %pad_maximum_fusion.4.refs_0_), channel_id=1, source_target_pairs={{0,4},{1,5},{2,6},{3,7},{4,8},{5,9},{6,10},{7,11},{8,12},{9,13},{1... | collective-permute-start | bytes 909320 | tf_op jit(solution)/shard_map/ppermute | solution.py:43
  15.9 7.7 %collective-permute-start.36 = (bf16[32,4736]{1,0:T(8,128)(2,1)S(1)}, bf16[32,4736]{1,0:T(8,128)(2,1)S(1)}, u32[]{:S(2)}, u32[]{:S(2)}) collective-permute-start(bf16[32,4736]{1,0:T(8,128)(2,1)S(1)} %pad_maximum_fusion.4.refs_0_), channel_id=1, source_target_pairs={{0,12},{1,13},{2,14},{3,15},{4,0},{5,1},{6,2},{7,3},{8,4},{9,5},{1... | collective-permute-start | bytes 909320 | tf_op jit(solution)/shard_map/ppermute | solution.py:43
  17.9 25.1 %copy-start = (bf16[512,2304]{1,0:T(8,128)(2,1)S(1)}, bf16[512,2304]{1,0:T(8,128)(2,1)}, u32[]{:S(2)}) copy-start(bf16[512,2304]{1,0:T(8,128)(2,1)} %cross_ref.3) | copy-start | bytes 7077892
  17.9 26.4 %copy-start.12 = (bf16[1,4608,512]{2,1,0:T(8,128)(2,1)S(1)}, bf16[1,4608,512]{2,1,0:T(8,128)(2,1)}, u32[]{:S(2)}) copy-start(bf16[1,4608,512]{2,1,0:T(8,128)(2,1)} %refs_4_.2) | copy-start | bytes 14155780
  23.6 26.6 %slice-start.2 = ((s8[4718592]{0:T(1024)(128)(4,1)}), s8[4194304]{0:T(1024)(128)(4,1)S(1)}, s32[]{:S(2)}) async-start(s8[4718592]{0:T(1024)(128)(4,1)} %bitcast.80), calls=%async_computation.2 | async-start | bytes 8388608
  25.3 10.8 %collective-permute-start.37 = (bf16[64,4736]{1,0:T(8,128)(2,1)S(1)}, bf16[64,4736]{1,0:T(8,128)(2,1)S(1)}, u32[]{:S(2)}, u32[]{:S(2)}) collective-permute-start(bf16[64,4736]{1,0:T(8,128)(2,1)S(1)} %get-tuple-element.127), channel_id=1, source_target_pairs={{0,2},{1,3},{2,0},{3,1},{4,6},{5,7},{6,4},{7,5},{8,10},{9,11},{10,... | collective-permute-start | bytes 1818632 | tf_op jit(solution)/shard_map/ppermute | solution.py:43
  28.0 14.6 %collective-permute-start.38 = (bf16[64,4736]{1,0:T(8,128)(2,1)S(1)}, bf16[64,4736]{1,0:T(8,128)(2,1)S(1)}, u32[]{:S(2)}, u32[]{:S(2)}) collective-permute-start(bf16[64,4736]{1,0:T(8,128)(2,1)S(1)} %get-tuple-element.128), channel_id=1, source_target_pairs={{0,1},{1,2},{2,3},{3,0},{4,5},{5,6},{6,7},{7,4},{8,9},{9,10},{10,1... | collective-permute-start | bytes 1818632 | tf_op jit(solution)/shard_map/ppermute | solution.py:43
  28.7 21.5 %slice-start.3 = ((s8[4718592]{0:T(1024)(128)(4,1)}), s8[524288]{0:T(1024)(128)(4,1)S(1)}, s32[]{:S(2)}) async-start(s8[4718592]{0:T(1024)(128)(4,1)} %bitcast.80), calls=%async_computation.3 | async-start | bytes 1048576
  28.7 14.3 %collective-permute-start.39 = (bf16[64,4736]{1,0:T(8,128)(2,1)S(1)}, bf16[64,4736]{1,0:T(8,128)(2,1)S(1)}, u32[]{:S(2)}, u32[]{:S(2)}) collective-permute-start(bf16[64,4736]{1,0:T(8,128)(2,1)S(1)} %get-tuple-element.129), channel_id=1, source_target_pairs={{0,3},{1,0},{2,1},{3,2},{4,7},{5,4},{6,5},{7,6},{8,11},{9,8},{10,9... | collective-permute-start | bytes 1818632 | tf_op jit(solution)/shard_map/ppermute | solution.py:43
  43.0 9.2 %collective-permute-start.41 = (bf16[512,2304]{1,0:T(8,128)(2,1)S(1)}, bf16[512,2304]{1,0:T(8,128)(2,1)S(1)}, u32[]{:S(2)}, u32[]{:S(2)}) collective-permute-start(bf16[512,2304]{1,0:T(8,128)(2,1)S(1)} %copy-done), channel_id=1, source_target_pairs={{0,64},{1,65},{2,66},{3,67},{4,68},{5,69},{6,70},{7,71},{8,72},{9,... | collective-permute-start | bytes 7077896 | tf_op jit(solution)/shard_map/ppermute | solution.py:55
  46.5 5.6 %collective-permute-start.40 = (bf16[256,640]{1,0:T(8,128)(2,1)S(1)}, bf16[256,640]{1,0:T(8,128)(2,1)S(1)}, u32[]{:S(2)}, u32[]{:S(2)}) collective-permute-start(bf16[256,640]{1,0:T(8,128)(2,1)S(1)} %get-tuple-element.135.codes_ref.own_ref), channel_id=1, source_target_pairs={{0,64},{64,0},{1,65},{65,1},{2,66},{66,2},{3,67},{67,3},{4,68},{68... | collective-permute-start | bytes 983048 | tf_op jit(solution)/shard_map/ppermute | solution.py:63
  52.2 76.9 %copy-start.2 = (bf16[512,2304]{1,0:T(8,128)(2,1)}, bf16[512,2304]{1,0:T(8,128)(2,1)S(1)}, u32[]{:S(2)}) copy-start(bf16[512,2304]{1,0:T(8,128)(2,1)S(1)} %collective-permute-done.41.cross_first_ref) | copy-start | bytes 7077892
  54.6 33.2 %copy-start.8 = (bf16[1,8,4608]{2,1,0:T(8,128)(2,1)S(1)}, bf16[1,8,4608]{2,1,0:T(8,128)(2,1)}, u32[]{:S(2)}) copy-start(bf16[1,8,4608]{2,1,0:T(8,128)(2,1)} %targets_ref.1) | copy-start | bytes 221188
  54.6 11.8 %collective-permute-start.42 = (bf16[64,5632]{1,0:T(8,128)(2,1)S(1)}, bf16[64,5632]{1,0:T(8,128)(2,1)S(1)}, u32[]{:S(2)}, u32[]{:S(2)}) collective-permute-start(bf16[64,5632]{1,0:T(8,128)(2,1)S(1)} %get-tuple-element.142), channel_id=1, source_target_pairs={{0,2},{1,3},{2,0},{3,1},{4,6},{5,7},{6,4},{7,5},{8,10},{9,11},{10,... | collective-permute-start | bytes 2162696 | tf_op jit(solution)/shard_map/ppermute | solution.py:43
  55.9 18.8 %collective-permute-start.43 = (bf16[64,5632]{1,0:T(8,128)(2,1)S(1)}, bf16[64,5632]{1,0:T(8,128)(2,1)S(1)}, u32[]{:S(2)}, u32[]{:S(2)}) collective-permute-start(bf16[64,5632]{1,0:T(8,128)(2,1)S(1)} %get-tuple-element.143), channel_id=1, source_target_pairs={{0,3},{1,0},{2,1},{3,2},{4,7},{5,4},{6,5},{7,6},{8,11},{9,8},{10,9... | collective-permute-start | bytes 2162696 | tf_op jit(solution)/shard_map/ppermute | solution.py:43
  57.7 16.9 %collective-permute-start.44 = (bf16[64,5632]{1,0:T(8,128)(2,1)S(1)}, bf16[64,5632]{1,0:T(8,128)(2,1)S(1)}, u32[]{:S(2)}, u32[]{:S(2)}) collective-permute-start(bf16[64,5632]{1,0:T(8,128)(2,1)S(1)} %get-tuple-element.144), channel_id=1, source_target_pairs={{0,1},{1,2},{2,3},{3,0},{4,5},{5,6},{6,7},{7,4},{8,9},{9,10},{10,1... | collective-permute-start | bytes 2162696 | tf_op jit(solution)/shard_map/ppermute | solution.py:43
  75.8 8.1 %collective-permute-start.45 = (bf16[32,5632]{1,0:T(8,128)(2,1)S(1)}, bf16[32,5632]{1,0:T(8,128)(2,1)S(1)}, u32[]{:S(2)}, u32[]{:S(2)}) collective-permute-start(bf16[32,5632]{1,0:T(8,128)(2,1)S(1)} %get-tuple-element.146), channel_id=1, source_target_pairs={{0,8},{1,9},{2,10},{3,11},{4,12},{5,13},{6,14},{7,15},{8,0},{9,1},... | collective-permute-start | bytes 1081352 | tf_op jit(solution)/shard_map/ppermute | solution.py:43
  77.6 10.2 %collective-permute-start.46 = (bf16[32,5632]{1,0:T(8,128)(2,1)S(1)}, bf16[32,5632]{1,0:T(8,128)(2,1)S(1)}, u32[]{:S(2)}, u32[]{:S(2)}) collective-permute-start(bf16[32,5632]{1,0:T(8,128)(2,1)S(1)} %get-tuple-element.147), channel_id=1, source_target_pairs={{0,12},{1,13},{2,14},{3,15},{4,0},{5,1},{6,2},{7,3},{8,4},{9,5},{1... | collective-permute-start | bytes 1081352 | tf_op jit(solution)/shard_map/ppermute | solution.py:43
  79.0 8.8 %collective-permute-start.47 = (bf16[32,5632]{1,0:T(8,128)(2,1)S(1)}, bf16[32,5632]{1,0:T(8,128)(2,1)S(1)}, u32[]{:S(2)}, u32[]{:S(2)}) collective-permute-start(bf16[32,5632]{1,0:T(8,128)(2,1)S(1)} %get-tuple-element.148), channel_id=1, source_target_pairs={{0,4},{1,5},{2,6},{3,7},{4,8},{5,9},{6,10},{7,11},{8,12},{9,13},{1... | collective-permute-start | bytes 1081352 | tf_op jit(solution)/shard_map/ppermute | solution.py:43
  88.5 7.7 %collective-permute-start.48 = (bf16[32,4864]{1,0:T(8,128)(2,1)S(1)}, bf16[32,4864]{1,0:T(8,128)(2,1)S(1)}, u32[]{:S(2)}, u32[]{:S(2)}) collective-permute-start(bf16[32,4864]{1,0:T(8,128)(2,1)S(1)} %get-tuple-element.150), channel_id=1, source_target_pairs={{0,32},{1,33},{2,34},{3,35},{4,36},{5,37},{6,38},{7,39},{8,40},{9,... | collective-permute-start | bytes 933896 | tf_op jit(solution)/shard_map/ppermute | solution.py:43
  90.4 9.1 %collective-permute-start.49 = (bf16[32,4864]{1,0:T(8,128)(2,1)S(1)}, bf16[32,4864]{1,0:T(8,128)(2,1)S(1)}, u32[]{:S(2)}, u32[]{:S(2)}) collective-permute-start(bf16[32,4864]{1,0:T(8,128)(2,1)S(1)} %get-tuple-element.151), channel_id=1, source_target_pairs={{0,16},{1,17},{2,18},{3,19},{4,20},{5,21},{6,22},{7,23},{8,24},{9,... | collective-permute-start | bytes 933896 | tf_op jit(solution)/shard_map/ppermute | solution.py:43
  91.6 8.0 %collective-permute-start.50 = (bf16[32,4864]{1,0:T(8,128)(2,1)S(1)}, bf16[32,4864]{1,0:T(8,128)(2,1)S(1)}, u32[]{:S(2)}, u32[]{:S(2)}) collective-permute-start(bf16[32,4864]{1,0:T(8,128)(2,1)S(1)} %get-tuple-element.152), channel_id=1, source_target_pairs={{0,48},{1,49},{2,50},{3,51},{4,52},{5,53},{6,54},{7,55},{8,56},{9,... | collective-permute-start | bytes 933896 | tf_op jit(solution)/shard_map/ppermute | solution.py:43
  100.2 7.5 %collective-permute-start.51 = (bf16[32,4608]{1,0:T(8,128)(2,1)S(1)}, bf16[32,4608]{1,0:T(8,128)(2,1)S(1)}, u32[]{:S(2)}, u32[]{:S(2)}) collective-permute-start(bf16[32,4608]{1,0:T(8,128)(2,1)S(1)} %get-tuple-element.153.refs_0_), channel_id=1, source_target_pairs={{0,8},{1,9},{2,10},{3,11},{4,12},{5,13},{6,14},{7,15},{8,0},{9,1},... | collective-permute-start | bytes 884744 | tf_op jit(solution)/shard_map/ppermute | solution.py:43
  102.0 8.8 %collective-permute-start.52 = (bf16[32,4608]{1,0:T(8,128)(2,1)S(1)}, bf16[32,4608]{1,0:T(8,128)(2,1)S(1)}, u32[]{:S(2)}, u32[]{:S(2)}) collective-permute-start(bf16[32,4608]{1,0:T(8,128)(2,1)S(1)} %get-tuple-element.153.refs_0_), channel_id=1, source_target_pairs={{0,4},{1,5},{2,6},{3,7},{4,8},{5,9},{6,10},{7,11},{8,12},{9,13},{1... | collective-permute-start | bytes 884744 | tf_op jit(solution)/shard_map/ppermute | solution.py:43
  103.2 7.6 %collective-permute-start.53 = (bf16[32,4608]{1,0:T(8,128)(2,1)S(1)}, bf16[32,4608]{1,0:T(8,128)(2,1)S(1)}, u32[]{:S(2)}, u32[]{:S(2)}) collective-permute-start(bf16[32,4608]{1,0:T(8,128)(2,1)S(1)} %get-tuple-element.153.refs_0_), channel_id=1, source_target_pairs={{0,12},{1,13},{2,14},{3,15},{4,0},{5,1},{6,2},{7,3},{8,4},{9,5},{1... | collective-permute-start | bytes 884744 | tf_op jit(solution)/shard_map/ppermute | solution.py:43
  112.1 10.7 %collective-permute-start.54 = (bf16[64,4608]{1,0:T(8,128)(2,1)S(1)}, bf16[64,4608]{1,0:T(8,128)(2,1)S(1)}, u32[]{:S(2)}, u32[]{:S(2)}) collective-permute-start(bf16[64,4608]{1,0:T(8,128)(2,1)S(1)} %get-tuple-element.155), channel_id=1, source_target_pairs={{0,2},{1,3},{2,0},{3,1},{4,6},{5,7},{6,4},{7,5},{8,10},{9,11},{10,... | collective-permute-start | bytes 1769480 | tf_op jit(solution)/shard_map/ppermute | solution.py:43
  112.8 16.2 %collective-permute-start.55 = (bf16[64,4608]{1,0:T(8,128)(2,1)S(1)}, bf16[64,4608]{1,0:T(8,128)(2,1)S(1)}, u32[]{:S(2)}, u32[]{:S(2)}) collective-permute-start(bf16[64,4608]{1,0:T(8,128)(2,1)S(1)} %get-tuple-element.156), channel_id=1, source_target_pairs={{0,1},{1,2},{2,3},{3,0},{4,5},{5,6},{6,7},{7,4},{8,9},{9,10},{10,1... | collective-permute-start | bytes 1769480 | tf_op jit(solution)/shard_map/ppermute | solution.py:43
  114.9 14.1 %collective-permute-start.56 = (bf16[64,4608]{1,0:T(8,128)(2,1)S(1)}, bf16[64,4608]{1,0:T(8,128)(2,1)S(1)}, u32[]{:S(2)}, u32[]{:S(2)}) collective-permute-start(bf16[64,4608]{1,0:T(8,128)(2,1)S(1)} %get-tuple-element.157), channel_id=1, source_target_pairs={{0,3},{1,0},{2,1},{3,2},{4,7},{5,4},{6,5},{7,6},{8,11},{9,8},{10,9... | collective-permute-start | bytes 1769480 | tf_op jit(solution)/shard_map/ppermute | solution.py:43
  131.3 7.8 %collective-permute-start.57 = (bf16[256,3328]{1,0:T(8,128)(2,1)S(1)}, bf16[256,3328]{1,0:T(8,128)(2,1)S(1)}, u32[]{:S(2)}, u32[]{:S(2)}) collective-permute-start(bf16[256,3328]{1,0:T(8,128)(2,1)S(1)} %cross_back.1), channel_id=1, source_target_pairs={{64,0},{65,1},{66,2},{67,3},{68,4},{69,5},{70,6},{71,7},{72,8},{73... | collective-permute-start | bytes 5111816 | tf_op jit(solution)/shard_map/ppermute | solution.py:59
  139.1 4.7 %copy-start.7 = (bf16[1,8,4608]{2,1,0:T(8,128)(2,1)S(1)}, bf16[1,8,4608]{2,1,0:T(8,128)(2,1)}, u32[]{:S(2)}) copy-start(bf16[1,8,4608]{2,1,0:T(8,128)(2,1)} %param.9) | copy-start | bytes 221188
  139.1 4.7 %copy-start.11 = (s32[1,8,8]{2,1,0:T(8,128)S(1)}, s32[1,8,8]{2,1,0:T(8,128)}, u32[]{:S(2)}) copy-start(s32[1,8,8]{2,1,0:T(8,128)} %param.15) | copy-start | bytes 772
